TPU v7x, 32 devices: a whole 2x2x4 slice. The times are simulated.
32 devices in a mesh: wide: 8 (over z, y), narrow: 2 (over x), rep: 2 (over core).
Axes of the slice: x: 2, y: 2, z: 4, core: 2. Of those that a mesh axis runs over, the one named last changes fastest.
Arguments:
- layer_input: bfloat16 [2, 32, 128, 44, 1024], P('rep', None, 'wide', 'narrow'), may hold values from -6 to 6
- output_cotangent: bfloat16 [2, 32, 128, 44, 1024], P('rep', None, 'wide', 'narrow'), may hold values from -6 to 6
- spectral_weight: bfloat16 [2, 1536, 24, 2, 32, 32], P('narrow', 'wide'), may hold values from -6 to 6
Outputs:
- input_gradient: bfloat16 [2, 32, 128, 44, 1024], P('rep', None, 'wide', 'narrow')
- weight_gradient: float32 [2, 1536, 24, 2, 32, 32], P('narrow', 'wide', 'rep')
All inputs are finite; a program needn't handle non-finite values.
Results may differ from a plain program's by a relative error of at most 0.012.
Values may be sent and summed in bfloat16 or wider, within the bound.
A program may use at most 256 MiB of HBM per device.

v0:
```python
import math

import jax
import jax.numpy as jnp
from jax import lax
from jax.sharding import PartitionSpec as P

MX = 12
MY = 12
MZ = 16
MT = 4
NX = 128
NY = 44
NZ = 64
NT = 16


def kept_waves(length, modes):
    indices = jnp.arange(2 * modes, dtype=jnp.int32)
    return jnp.where(indices < modes, indices, indices + length - 2 * modes)


def phase_pair(length, modes):
    positions = jnp.arange(length, dtype=jnp.int32)
    phase_turns = positions[:, None] * kept_waves(length, modes)[None, :] % length
    phases = 2.0 * math.pi / length * phase_turns.astype(jnp.float32)
    return (jnp.cos(phases), jnp.sin(phases))


def forward_table(length, modes):
    cosine, sine_part = phase_pair(length, modes)
    twiddle = jnp.stack(
        [jnp.stack([cosine, -sine_part], axis=-1), jnp.stack([sine_part, cosine], axis=-1)], axis=1
    )
    return twiddle.astype(jnp.bfloat16)


def inverse_table(length, modes):
    cosine, sine_part = phase_pair(length, modes)
    cos_rows = cosine.T
    sin_rows = sine_part.T
    twiddle = jnp.stack(
        [jnp.stack([cos_rows, sin_rows], axis=-1), jnp.stack([-sin_rows, cos_rows], axis=-1)],
        axis=1,
    )
    return twiddle.astype(jnp.bfloat16)


def plane_tables():
    positions = jnp.arange(NZ * NT, dtype=jnp.int32)
    depth_index = positions // NT
    moment = positions % NT
    pair_index = jnp.arange(2 * MZ * MT, dtype=jnp.int32)
    wave_z = kept_waves(NZ, MZ)[pair_index // MT]
    wave_t = pair_index % MT
    phase_turns = (
        depth_index[:, None] * wave_z[None, :] % NZ * NT
        + moment[:, None] * wave_t[None, :] % NT * NZ
    ) % (NZ * NT)
    phases = 2.0 * math.pi / (NZ * NT) * phase_turns.astype(jnp.float32)
    norm_scale = 1.0 / math.sqrt(NX * NY * NZ * NT)
    cosine = norm_scale * jnp.cos(phases)
    sine_part = norm_scale * jnp.sin(phases)
    forward = jnp.concatenate([cosine, -sine_part], axis=1).astype(jnp.bfloat16)
    inverse = jnp.concatenate([cosine.T, -sine_part.T], axis=0).astype(jnp.bfloat16)
    doubled = jnp.where(wave_t == 0, 1.0, 2.0).astype(jnp.float32)
    factor = jnp.concatenate([doubled, doubled])
    return (forward, inverse, factor)


def outer_terms(input_spec, grad_spec):
    in_real = input_spec[..., 0, :].astype(jnp.float32)[..., :, None]
    in_imag = input_spec[..., 1, :].astype(jnp.float32)[..., :, None]
    grad_real = grad_spec[..., 0, :].astype(jnp.float32)[..., None, :]
    grad_imag = grad_spec[..., 1, :].astype(jnp.float32)[..., None, :]
    real_part = in_real * grad_real + in_imag * grad_imag
    imag_part = in_real * grad_imag - in_imag * grad_real
    return jnp.stack([real_part, imag_part], axis=-3)


def shards(layer_input, output_cotangent, spectral_weight):
    input_field = layer_input[0]
    grad_field = output_cotangent[0]
    channels, local_x, local_y, plane_cells = grad_field.shape
    pair_count = 2 * MZ * MT
    forward, inverse, factor = plane_tables()
    input_plane = jnp.dot(
        input_field.reshape(-1, plane_cells), forward, preferred_element_type=jnp.float32
    )
    input_plane = input_plane.astype(jnp.bfloat16).reshape(
        channels, local_x, local_y, 2, pair_count
    )
    grad_plane = (
        jnp.dot(grad_field.reshape(-1, plane_cells), forward, preferred_element_type=jnp.float32)
        * factor
    )
    grad_plane = grad_plane.astype(jnp.bfloat16).reshape(channels, local_x, local_y, 2, pair_count)
    table_y = forward_table(NY, MY)
    fields = (
        lax.all_to_all(input_plane, "narrow", split_axis=4, concat_axis=2, tiled=True),
        lax.all_to_all(grad_plane, "narrow", split_axis=4, concat_axis=2, tiled=True),
    )
    input_line, grad_line = tuple(
        (
            jnp.einsum(
                "cxyrm,yrjs->cxsjm", field, table_y, preferred_element_type=jnp.float32
            ).astype(jnp.bfloat16)
            for field in fields
        )
    )
    combos = input_line.shape[3] * input_line.shape[4]
    input_flat = input_line.reshape(channels, local_x, 2, combos)
    grad_flat = grad_line.reshape(channels, local_x, 2, combos)
    table_x = forward_table(NX, MX)
    back_table_x = inverse_table(NX, MX)
    back_table_y = inverse_table(NY, MY)
    fields = (
        lax.all_to_all(input_flat, "wide", split_axis=3, concat_axis=1, tiled=True),
        lax.all_to_all(grad_flat, "wide", split_axis=3, concat_axis=1, tiled=True),
    )
    input_spec, grad_spec = tuple(
        (
            jnp.einsum(
                "cxrq,xrks->qksc", field, table_x, preferred_element_type=jnp.float32
            ).astype(jnp.bfloat16)
            for field in fields
        )
    )
    weight_block = spectral_weight[0]
    weight_real = weight_block[:, :, 0]
    weight_imag = weight_block[:, :, 1]
    grad_real = grad_spec[:, :, 0]
    grad_imag = grad_spec[:, :, 1]

    def contract(left, right):
        return jnp.einsum("qkio,qko->qki", left, right, preferred_element_type=jnp.float32)

    dual_real = contract(weight_real, grad_real) + contract(weight_imag, grad_imag)
    dual_imag = contract(weight_real, grad_imag) - contract(weight_imag, grad_real)
    dual = jnp.stack([dual_real, dual_imag], axis=2).astype(jnp.bfloat16)
    both_input, both_grad = (
        lax.all_gather(input_spec[None], "rep", axis=0, tiled=True),
        lax.all_gather(grad_spec[None], "rep", axis=0, tiled=True),
    )
    half_modes = input_spec.shape[1] // lax.axis_size("rep")
    mode_start = lax.axis_index("rep") * half_modes
    input_half = lax.dynamic_slice_in_dim(both_input, mode_start, half_modes, 2)
    grad_half = lax.dynamic_slice_in_dim(both_grad, mode_start, half_modes, 2)
    weight_grad = jnp.sum(outer_terms(input_half, grad_half), axis=0)
    back_x = jnp.einsum(
        "qksc,ksxr->cxrq", dual, back_table_x, preferred_element_type=jnp.float32
    ).astype(jnp.bfloat16)
    block_part = lax.all_to_all(back_x, "wide", split_axis=1, concat_axis=3, tiled=True)
    shaped = block_part.reshape(block_part.shape[0], local_x, 2, 2 * MY, -1)
    back_line = jnp.einsum(
        "cxsjm,jsyr->cxyrm", shaped, back_table_y, preferred_element_type=jnp.float32
    ).astype(jnp.bfloat16)
    block_part = lax.all_to_all(back_line, "narrow", split_axis=2, concat_axis=4, tiled=True)
    result = jnp.dot(
        block_part.reshape(-1, 2 * pair_count), inverse, preferred_element_type=jnp.float32
    )
    input_grad = result.astype(jnp.bfloat16).reshape(
        block_part.shape[0], local_x, local_y, plane_cells
    )
    return (input_grad[None], weight_grad[None])


def solution(mesh):
    in_specs = (
        P("rep", None, "wide", "narrow", None),
        P("rep", None, "wide", "narrow", None),
        P("narrow", "wide", None, None, None, None),
    )
    out_specs = (
        P("rep", None, "wide", "narrow", None),
        P("narrow", "wide", "rep", None, None, None),
    )
    return jax.shard_map(shards, mesh=mesh, in_specs=in_specs, out_specs=out_specs, check_vma=False)
```

profile of v0, /device:TPU:0, one launch (start us, length us, event | category | flops | bytes accessed | tf_op | source)
XLA Modules:
  0.0 1012.2 jit_solution(7817657932212851413)
XLA Ops:
  7.3 26.5 %copy.143 = bf16[1,32,16,22,1024]{4,3,2,1,0:T(8,128)(2,1)} copy(bf16[1,32,16,22,1024]{4,2,3,1,0:T(8,128)(2,1)} %param.4) | data formatting | bytes 46137344 | tf_op args[1]
  33.8 33.0 %reshape_squeeze.6 = bf16[11264,1024]{1,0:T(8,128)(2,1)} reshape(bf16[1,32,16,22,1024]{4,3,2,1,0:T(8,128)(2,1)} %copy.143) | data formatting | bytes 46137344 | tf_op jit(solution)/shard_map/reshape;squeeze | solution.py:94
  71.1 12.7 %fusion.6 = bf16[11264,256]{0,1:T(8,128)(2,1)} fusion(bf16[11264,1024]{1,0:T(8,128)(2,1)} %reshape_squeeze.6, f32[256]{0:T(256)S(1)} %pad_maximum_fusion.3, bf16[1024,128]{1,0:T(8,128)(2,1)S(1)} %get-tuple-element.31, bf16[1024,128]{1,0:T(8,128)(2,1)S(1)} %get-tuple-element.30), kind=kOutput, calls=%fused_computation.18 | convolution fusion | flops 5912395776 | bytes 29361152 | tf_op jit(solution)/shard_map/dot_general | solution.py:94
  83.8 8.3 copy.144
  92.1 9.1 reshape.616
  101.2 37.4 %copy.145 = bf16[32,16,22,2,128]{0,1,3,2,4:T(8,128)(2,1)} copy(bf16[32,16,22,2,128]{4,3,2,1,0:T(2,128)(2,1)} %reshape.616) | data formatting | bytes 11534336 | tf_op jit(solution)/shard_map/reshape | solution.py:97
  138.6 33.3 %reshape.661 = bf16[2,2,720896]{2,1,0:T(2,128)(2,1)} reshape(bf16[128,22,2,16,32]{4,3,2,1,0:T(8,128)(2,1)} %bitcast.211) | data formatting | bytes 11534336
  178.1 26.7 %copy.159 = bf16[1,32,16,22,1024]{4,3,2,1,0:T(8,128)(2,1)} copy(bf16[1,32,16,22,1024]{4,2,3,1,0:T(8,128)(2,1)} %param.3) | data formatting | bytes 46137344 | tf_op args[0]
  204.8 33.0 %reshape_squeeze.7 = bf16[11264,1024]{1,0:T(8,128)(2,1)} reshape(bf16[1,32,16,22,1024]{4,3,2,1,0:T(8,128)(2,1)} %copy.159) | data formatting | bytes 46137344 | tf_op jit(solution)/shard_map/reshape;squeeze | solution.py:88
  237.8 12.4 %fusion.5 = bf16[11264,256]{0,1:T(8,128)(2,1)} fusion(bf16[11264,1024]{1,0:T(8,128)(2,1)} %reshape_squeeze.7, bf16[1024,128]{1,0:T(8,128)(2,1)S(1)} %get-tuple-element.31, bf16[1024,128]{1,0:T(8,128)(2,1)S(1)} %get-tuple-element.30), kind=kOutput, calls=%fused_computation.17 | convolution fusion | flops 5909512192 | bytes 29360128 | tf_op jit(solution)/shard_map/dot_general | solution.py:87
  250.1 8.3 copy.160
  258.4 9.1 reshape.620
  267.5 37.4 %copy.161 = bf16[32,16,22,2,128]{0,1,3,2,4:T(8,128)(2,1)} copy(bf16[32,16,22,2,128]{4,3,2,1,0:T(2,128)(2,1)} %reshape.620) | data formatting | bytes 11534336 | tf_op jit(solution)/shard_map/reshape | solution.py:90
  304.9 33.5 %reshape.667 = bf16[2,2,720896]{2,1,0:T(2,128)(2,1)} reshape(bf16[128,22,2,16,32]{4,3,2,1,0:T(8,128)(2,1)} %bitcast.212) | data formatting | bytes 11534336
  344.8 24.6 %reshape.662 = bf16[128,22,2,16,32]{4,3,2,1,0:T(8,128)(2,1)} reshape(bf16[2,2,720896]{2,1,0:T(2,128)(2,1)} %all-to-all-done) | data formatting | bytes 11534336
  369.4 42.2 %copy.212 = bf16[32,16,22,2,2,64]{5,4,1,3,2,0:T(2,128)(2,1)} copy(bf16[32,16,22,2,2,64]{0,1,3,2,5,4:T(8,128)(2,1)} %bitcast.213) | data formatting | bytes 11534336 | tf_op jit(solution)/shard_map/all_to_all | solution.py:101
  411.6 7.0 copy.147
  418.6 6.9 fusion.14
  425.5 15.9 %copy.213 = bf16[32,16,2,24,64]{0,1,2,4,3:T(8,128)(2,1)} copy(bf16[32,16,2,24,64]{4,3,1,0,2:T(8,128)(2,1)} %fusion.14) | data formatting | bytes 6291456 | tf_op jit(solution)/shard_map/reshape | solution.py:113
  441.4 14.5 %reshape.663 = bf16[8,2,98304]{2,1,0:T(2,128)(2,1)} reshape(bf16[1536,2,16,32]{3,2,1,0:T(8,128)(2,1)} %bitcast.217) | data formatting | bytes 6291456
  456.0 7.5 all-to-all-start.1
  463.5 24.5 %reshape.668 = bf16[128,22,2,16,32]{4,3,2,1,0:T(8,128)(2,1)} reshape(bf16[2,2,720896]{2,1,0:T(2,128)(2,1)} %all-to-all-done.4) | data formatting | bytes 11534336
  488.0 42.2 %copy.219 = bf16[32,16,22,2,2,64]{5,4,1,3,2,0:T(2,128)(2,1)} copy(bf16[32,16,22,2,2,64]{0,1,3,2,5,4:T(8,128)(2,1)} %bitcast.214) | data formatting | bytes 11534336 | tf_op jit(solution)/shard_map/all_to_all | solution.py:100
  530.1 7.0 copy.163
  537.2 6.9 fusion.15
  544.1 15.9 %copy.220 = bf16[32,16,2,24,64]{0,1,2,4,3:T(8,128)(2,1)} copy(bf16[32,16,2,24,64]{4,3,1,0,2:T(8,128)(2,1)} %fusion.15) | data formatting | bytes 6291456 | tf_op jit(solution)/shard_map/reshape | solution.py:112
  560.0 14.5 %reshape.669 = bf16[8,2,98304]{2,1,0:T(2,128)(2,1)} reshape(bf16[1536,2,16,32]{3,2,1,0:T(8,128)(2,1)} %bitcast.218) | data formatting | bytes 6291456
  574.5 6.5 all-to-all-start.5
  581.3 10.6 %reshape.664 = bf16[1536,2,16,32]{3,2,1,0:T(8,128)(2,1)} reshape(bf16[8,2,98304]{2,1,0:T(2,128)(2,1)} %all-to-all-done.1) | data formatting | bytes 6291456
  591.9 15.9 %copy.151 = bf16[32,8,16,2,192]{4,2,1,3,0:T(8,128)(2,1)} copy(bf16[32,8,16,2,192]{0,2,3,4,1:T(8,128)(2,1)} %bitcast.219) | data formatting | bytes 6291456 | tf_op jit(solution)/shard_map/all_to_all | solution.py:119
  612.4 25.4 %fusion = (f32[192,24,32]{0,2,1:T(8,128)S(1)}, f32[192,24,32]{0,2,1:T(8,128)S(1)}, f32[192,24,32]{0,2,1:T(8,128)S(1)}, f32[192,24,32]{0,2,1:T(8,128)S(1)}) fusion(f32[192,24,32]{0,2,1:T(8,128)S(1)} %copy.224, bf16[192,24,2,32,32]{0,4,3,2,1:T(8,128)(2,1)} %bitcast.225, f32[192,24,32]{0,2,1:T(8,128)S(1)} %copy.225), kind=kLoop, calls=%fused_computation.6 | loop fusion | flops 46596096 | bytes 22413312
  659.6 10.8 %reshape.670 = bf16[1536,2,16,32]{3,2,1,0:T(8,128)(2,1)} reshape(bf16[8,2,98304]{2,1,0:T(2,128)(2,1)} %all-to-all-done.5) | data formatting | bytes 6291456
  670.4 16.2 %copy.167 = bf16[32,8,16,2,192]{4,2,1,3,0:T(8,128)(2,1)} copy(bf16[32,8,16,2,192]{0,2,3,4,1:T(8,128)(2,1)} %bitcast.220) | data formatting | bytes 6291456 | tf_op jit(solution)/shard_map/all_to_all | solution.py:118
  718.6 29.6 %all-to-all-done.2 = bf16[32,128,2,192]{3,0,2,1:T(8,128)(2,1)} async-done(((bf16[32,128,2,192]{3,0,2,1:T(8,128)(2,1)}), bf16[32,128,2,192]{3,0,2,1:T(8,128)(2,1)}, u32[]{:S(2)}, u32[]{:S(2)}) %all-to-all-start.2) | async-done | bytes 3145760 | tf_op jit(solution)/shard_map/all_to_all | solution.py:153
  748.3 6.6 copy.155
  754.9 9.5 reshape.654
  764.3 9.6 fusion.7
  773.9 12.2 %copy.255 = bf16[32,16,44,2,64]{4,1,3,0,2:T(8,128)(2,1)} copy(bf16[32,16,44,2,64]{4,2,1,0,3:T(8,128)(2,1)} %fusion.7) | data formatting | bytes 11534336 | tf_op jit(solution)/shard_map/convert_element_type | solution.py:157
  786.2 17.5 %reshape.665 = bf16[2,2,720896]{2,1,0:T(2,128)(2,1)} reshape(bf16[44,32,2,16,64]{4,3,2,1,0:T(8,128)(2,1)} %bitcast.223) | data formatting | bytes 11534336
  809.8 17.3 %multiply_add_fusion = (f32[2,192,12,1,32,32]{1,5,4,3,2,0:T(8,128)}, f32[2,192,12,1,32,32]{1,5,4,3,2,0:T(8,128)}) fusion(f32[2,192,12,32]{1,3,2,0:T(8,128)S(1)} %copy-done.2, f32[2,192,12,32]{1,3,2,0:T(8,128)S(1)} %copy-done.4, f32[2,192,12,32]{1,3,2,0:T(8,128)S(1)} %copy-done.1, f32[2,192,12,32]{1,3,2,0:T(8,128)S(1)} %copy-done.3), kind=kLoop, calls=%fused_computation.12 | loop fusion | flops 28311552 | bytes 40108032 | tf_op jit(solution)/shard_map/add | solution.py:76
  827.2 30.1 %maximum_reduce_fusion = f32[192,12,2,32,32]{0,4,3,2,1:T(8,128)} fusion(f32[2,192,12,1,32,32]{1,5,4,3,2,0:T(8,128)} %get-tuple-element.25, f32[2,192,12,1,32,32]{1,5,4,3,2,0:T(8,128)} %get-tuple-element.24), kind=kLoop, calls=%fused_computation.1 | loop fusion | flops 14155776 | bytes 56623104 | tf_op jit(solution)/shard_map/reduce_sum | solution.py:149
  857.3 15.3 %all-to-all-done.3 = bf16[2,2,720896]{2,1,0:T(2,128)(2,1)} async-done(((bf16[2,2,720896]{2,1,0:T(2,128)(2,1)}), bf16[2,2,720896]{2,1,0:T(2,128)(2,1)}, u32[]{:S(2)}, u32[]{:S(2)}) %all-to-all-start.3) | async-done | bytes 5767200 | tf_op jit(solution)/shard_map/all_to_all | solution.py:158
  872.5 17.2 %reshape.666 = bf16[44,32,2,16,64]{4,3,2,1,0:T(8,128)(2,1)} reshape(bf16[2,2,720896]{2,1,0:T(2,128)(2,1)} %all-to-all-done.3) | data formatting | bytes 11534336
  889.8 21.7 %copy.158 = bf16[32,16,22,2,2,64]{5,4,3,2,1,0:T(2,128)(2,1)} copy(bf16[32,16,22,2,2,64]{5,1,3,0,2,4:T(8,128)(2,1)} %bitcast.224) | data formatting | bytes 11534336 | tf_op jit(solution)/shard_map/all_to_all | solution.py:158
  911.4 20.9 %reshape.619 = bf16[11264,256]{1,0:T(8,128)(2,1)} reshape(bf16[32,16,22,2,2,64]{5,4,3,2,1,0:T(2,128)(2,1)} %copy.158) | data formatting | bytes 11534336 | tf_op jit(solution)/shard_map/reshape | solution.py:160
  932.3 14.3 %convolution_convert_fusion = bf16[11264,1024]{1,0:T(8,128)(2,1)} fusion(bf16[11264,256]{1,0:T(8,128)(2,1)} %reshape.619, bf16[128,1024]{1,0:T(8,128)(2,1)S(1)} %copy-done.5, bf16[128,1024]{1,0:T(8,128)(2,1)S(1)} %get-tuple-element.28), kind=kOutput, calls=%fused_computation.13 | convolution fusion | flops 5918162944 | bytes 29360128 | tf_op jit(solution)/shard_map/dot_general | solution.py:159
  946.7 32.9 %broadcast_in_dim_reshape.3 = bf16[1,32,16,22,1024]{4,3,2,1,0:T(8,128)(2,1)} reshape(bf16[11264,1024]{1,0:T(8,128)(2,1)} %convolution_convert_fusion) | data formatting | bytes 46137344 | tf_op jit(solution)/shard_map/broadcast_in_dim;reshape | solution.py:165
  979.6 25.3 %copy.175 = bf16[1,32,16,22,1024]{4,2,3,1,0:T(8,128)(2,1)} copy(bf16[1,32,16,22,1024]{4,3,2,1,0:T(8,128)(2,1)} %broadcast_in_dim_reshape.3) | data formatting | bytes 46137344
  (79 shorter events, 81.3 us)
Async XLA Ops:
  7.2 60.8 %copy-start.6 = (s32[1024]{0:T(1024)}, s32[1024]{0:T(1024)S(1)}, u32[]{:S(2)}) copy-start(s32[1024]{0:T(1024)S(1)} %get-tuple-element.52) | copy-start | bytes 12292
  7.2 60.8 %copy-start.8 = (s32[1024]{0:T(1024)}, s32[1024]{0:T(1024)S(1)}, u32[]{:S(2)}) copy-start(s32[1024]{0:T(1024)S(1)} %get-tuple-element.53) | copy-start | bytes 12292
  7.2 60.8 %copy-start.12 = (s32[128]{0:T(128)}, s32[128]{0:T(128)S(1)}, u32[]{:S(2)}) copy-start(s32[128]{0:T(128)S(1)} %and_select_fusion) | copy-start | bytes 1540
  68.0 15.8 %copy-start.10 = (s32[128]{0:T(128)}, s32[128]{0:T(128)S(1)}, u32[]{:S(2)}) copy-start(s32[128]{0:T(128)S(1)} %gather_fusion) | copy-start | bytes 1540
  171.9 166.6 %all-to-all-start = ((bf16[2,2,720896]{2,1,0:T(2,128)(2,1)}), bf16[2,2,720896]{2,1,0:T(2,128)(2,1)}, u32[]{:S(2)}, u32[]{:S(2)}) async-start(bf16[2,2,720896]{2,1,0:T(2,128)(2,1)} %reshape.661), calls=%async_computation | async-start | bytes 11534336 | tf_op jit(solution)/shard_map/all_to_all | solution.py:101
  338.5 117.5 %all-to-all-start.4 = ((bf16[2,2,720896]{2,1,0:T(2,128)(2,1)}), bf16[2,2,720896]{2,1,0:T(2,128)(2,1)}, u32[]{:S(2)}, u32[]{:S(2)}) async-start(bf16[2,2,720896]{2,1,0:T(2,128)(2,1)} %reshape.667), calls=%async_computation.4 | async-start | bytes 11534336 | tf_op jit(solution)/shard_map/all_to_all | solution.py:100
  456.0 118.6 %all-to-all-start.1 = ((bf16[8,2,98304]{2,1,0:T(2,128)(2,1)}), bf16[8,2,98304]{2,1,0:T(2,128)(2,1)}, u32[]{:S(2)}, u32[]{:S(2)}) async-start(bf16[8,2,98304]{2,1,0:T(2,128)(2,1)} %reshape.663), calls=%async_computation.1 | async-start | bytes 6291456 | tf_op jit(solution)/shard_map/all_to_all | solution.py:119
  574.5 76.6 %all-to-all-start.5 = ((bf16[8,2,98304]{2,1,0:T(2,128)(2,1)}), bf16[8,2,98304]{2,1,0:T(2,128)(2,1)}, u32[]{:S(2)}, u32[]{:S(2)}) async-start(bf16[8,2,98304]{2,1,0:T(2,128)(2,1)} %reshape.669), calls=%async_computation.5 | async-start | bytes 6291456 | tf_op jit(solution)/shard_map/all_to_all | solution.py:118
  610.9 0.9 copy-start
  651.2 97.1 %all-to-all-start.2 = ((bf16[32,128,2,192]{3,0,2,1:T(8,128)(2,1)}), bf16[32,128,2,192]{3,0,2,1:T(8,128)(2,1)}, u32[]{:S(2)}, u32[]{:S(2)}) async-start(bf16[32,128,2,192]{3,0,2,1:T(8,128)(2,1)} %copy.153), calls=%async_computation.2 | async-start | bytes 8388608 | tf_op jit(solution)/shard_map/all_to_all | solution.py:153
  655.7 40.1 %all-gather.7.cloned.1.call-start = ((), (), s32[]{:S(2)}) async-start(), calls=%async_computation.7 | async-start | bytes 7077888 | tf_op jit(solution)/shard_map/all_gather | solution.py:143
  659.5 48.7 %all-gather.5.cloned.1.call-start = ((), (), s32[]{:S(2)}) async-start(), calls=%async_computation.6 | async-start | bytes 7077888 | tf_op jit(solution)/shard_map/all_gather | solution.py:142
  670.4 21.9 %copy-start.7 = (s32[1024]{0:T(1024)S(1)}, s32[1024]{0:T(1024)}, u32[]{:S(2)}) copy-start(s32[1024]{0:T(1024)} %copy-done.6) | copy-start | bytes 12292
  670.4 21.9 %copy-start.9 = (s32[1024]{0:T(1024)S(1)}, s32[1024]{0:T(1024)}, u32[]{:S(2)}) copy-start(s32[1024]{0:T(1024)} %copy-done.8) | copy-start | bytes 12292
  670.4 21.9 %copy-start.11 = (s32[128]{0:T(128)S(1)}, s32[128]{0:T(128)}, u32[]{:S(2)}) copy-start(s32[128]{0:T(128)} %copy-done.10) | copy-start | bytes 1540
  670.4 21.9 %copy-start.13 = (s32[128]{0:T(128)S(1)}, s32[128]{0:T(128)}, u32[]{:S(2)}) copy-start(s32[128]{0:T(128)} %copy-done.12) | copy-start | bytes 1540
  786.2 23.6 %copy-start.1 = (f32[2,192,12,32]{1,3,2,0:T(8,128)S(1)}, f32[2,192,12,32]{1,3,2,0:T(8,128)}, u32[]{:S(2)}) copy-start(f32[2,192,12,32]{1,3,2,0:T(8,128)} %copy.172) | copy-start | bytes 1769476
  786.2 23.6 %copy-start.2 = (f32[2,192,12,32]{1,3,2,0:T(8,128)S(1)}, f32[2,192,12,32]{1,3,2,0:T(8,128)}, u32[]{:S(2)}) copy-start(f32[2,192,12,32]{1,3,2,0:T(8,128)} %copy.174) | copy-start | bytes 1769476
  786.2 23.6 %copy-start.3 = (f32[2,192,12,32]{1,3,2,0:T(8,128)S(1)}, f32[2,192,12,32]{1,3,2,0:T(8,128)}, u32[]{:S(2)}) copy-start(f32[2,192,12,32]{1,3,2,0:T(8,128)} %copy.170) | copy-start | bytes 1769476
  786.2 23.6 %copy-start.4 = (f32[2,192,12,32]{1,3,2,0:T(8,128)S(1)}, f32[2,192,12,32]{1,3,2,0:T(8,128)}, u32[]{:S(2)}) copy-start(f32[2,192,12,32]{1,3,2,0:T(8,128)} %copy.173) | copy-start | bytes 1769476
  803.7 68.8 %all-to-all-start.3 = ((bf16[2,2,720896]{2,1,0:T(2,128)(2,1)}), bf16[2,2,720896]{2,1,0:T(2,128)(2,1)}, u32[]{:S(2)}, u32[]{:S(2)}) async-start(bf16[2,2,720896]{2,1,0:T(2,128)(2,1)} %reshape.665), calls=%async_computation.3 | async-start | bytes 11534336 | tf_op jit(solution)/shard_map/all_to_all | solution.py:158
  911.4 20.9 %copy-start.5 = (bf16[128,1024]{1,0:T(8,128)(2,1)S(1)}, bf16[128,1024]{1,0:T(8,128)(2,1)}, u32[]{:S(2)}) copy-start(bf16[128,1024]{1,0:T(8,128)(2,1)} %get-tuple-element.29) | copy-start | bytes 786436
Sparse Core Ops, SparseCore 0:
  659.6 15.9 all-gather.6
  692.3 15.8 all-gather.4
where the time goes:
time: 1030 us; the launch traced here: 1010 us
  local copies, waits for them, and re-layouts  747 us (73%)
  other arithmetic  92.1 us (9%)
  matrix products  69.8 us (7%)
  waiting for transfers between devices  51.6 us (5%)
  starting transfers between devices  37 us (4%)
  between operations  14.9 us (1%)
    unnamed x43, local copies, waits for them, and re-layouts  281 us
    all_to_all x2, local copies, waits for them, and re-layouts, shards(): lax.all_to_all(grad_plane, 'narrow', split_axis=4, concat_axis=2, tiled=T...  49.2 us
    all_to_all x2, local copies, waits for them, and re-layouts, shards(): lax.all_to_all(input_plane, 'narrow', split_axis=4, concat_axis=2, tiled=...  49.2 us
    reshape x2, local copies, waits for them, and re-layouts, shards(): grad_plane.astype(jnp.bfloat16)  46.5 us
    reshape x2, local copies, waits for them, and re-layouts, shards(): input_plane.astype(jnp.bfloat16)  46.5 us
    another operation x1, local copies, waits for them, and re-layouts, shards(): grad_field.reshape(-1, plane_cells)  33 us
    another operation x1, local copies, waits for them, and re-layouts, shards(): input_field.reshape(-1, plane_cells)  33 us
    another operation x1, local copies, waits for them, and re-layouts, shards(): return (input_grad[None], weight_grad[None])  32.9 us
  transfers between devices with their start and end apart: 8, of which 4 were waited for; matrix products, arithmetic and copies ran while one was open for 55% of the time, Pallas kernels for 0%

commit v1 on v0

--- a/solution.py
+++ b/solution.py
@@ -1,8 +1,13 @@
+import functools
 import math
 
 import jax
 import jax.numpy as jnp
+import ml_dtypes
+import numpy as np
 from jax import lax
+from jax.experimental import pallas as pl
+from jax.experimental.pallas import tpu as pltpu
 from jax.sharding import PartitionSpec as P
 
 MX = 12
@@ -13,6 +18,13 @@
 NY = 44
 NZ = 64
 NT = 16
+
+CHANNEL_STEP = 4
+SPEC_STEP = 16
+GRAD_CHUNKS = 1
+INPUT_CHUNKS = 1
+BACK_CHUNKS = 1
+VMEM_BYTES = 48 * 1024 * 1024
 
 
 def kept_waves(length, modes):
@@ -165,6 +177,459 @@
     return (input_grad[None], weight_grad[None])
 
 
+def np_phases(length, modes):
+    waves = np.arange(2 * modes)
+    waves = np.where(waves < modes, waves, waves + length - 2 * modes)
+    turns = np.arange(length)[:, None] * waves[None, :] % length
+    phases = np.float32(2.0 * math.pi / length) * turns.astype(np.float32)
+    return (np.cos(phases), np.sin(phases))
+
+
+def np_plane(blocks):
+    positions = np.arange(NZ * NT)
+    pairs = np.arange(2 * MZ * MT)
+    waves = np.arange(2 * MZ)
+    waves = np.where(waves < MZ, waves, waves + NZ - 2 * MZ)[pairs // MT]
+    moments = pairs % MT
+    turns = (
+        (positions // NT)[:, None] * waves[None, :] % NZ * NT
+        + (positions % NT)[:, None] * moments[None, :] % NT * NZ
+    ) % (NZ * NT)
+    phases = np.float32(2.0 * math.pi / (NZ * NT)) * turns.astype(np.float32)
+    scale = np.float32(1.0 / math.sqrt(NX * NY * NZ * NT))
+    cells = NZ * NT
+    cosine = (scale * np.cos(phases)).reshape(cells, blocks, -1)
+    sine = (scale * np.sin(phases)).reshape(cells, blocks, -1)
+    factor = np.where(moments == 0, 1.0, 2.0).astype(np.float32).reshape(blocks, -1)
+    return cosine, sine, factor
+
+
+def pick(options, index):
+    return lax.dynamic_index_in_dim(jnp.asarray(np.stack(options)), index, 0, keepdims=False)
+
+
+def bf16(array):
+    return np.asarray(array, np.float32).astype(ml_dtypes.bfloat16)
+
+
+def zt_tables(order):
+    cosine, sine, factor = np_plane(len(order))
+    both = np.stack([cosine, -sine], axis=2)[:, order]
+    plain = bf16(both)
+    grad = bf16(plain.astype(np.float32) * factor[order][None, :, None, :])
+    cells = both.shape[0]
+    plain = plain.reshape(cells, -1)
+    return plain, grad.reshape(cells, -1), np.ascontiguousarray(plain.T)
+
+
+def y_tables(order, local_y, local_x):
+    cosine, sine = np_phases(NY, MY)
+    both = bf16(np.stack([cosine, sine])).astype(np.float32)
+    rows = np.concatenate([np.arange(o * local_y, (o + 1) * local_y) for o in order])
+    both = both[:, rows]
+    eye = np.eye(local_x, dtype=np.float32)
+    forward = np.einsum("ayj,xz->ajxyz", both, eye).reshape(2 * 2 * MY * local_x, -1)
+    back = np.einsum("ayj,xz->ayxjz", both, eye).reshape(2 * NY * local_x, -1)
+    return bf16(forward), bf16(back)
+
+
+def x_tables():
+    cosine, sine = np_phases(NX, MX)
+    forward = np.concatenate([cosine.T, sine.T], axis=0)
+    back = np.concatenate([cosine, sine], axis=0)
+    return bf16(forward), bf16(back)
+
+
+def params():
+    return pltpu.CompilerParams(vmem_limit_bytes=VMEM_BYTES)
+
+
+def cost(flops, moved):
+    return pl.CostEstimate(flops=int(flops), bytes_accessed=int(moved), transcendentals=0)
+
+
+def signs(shape, first):
+    lane = lax.broadcasted_iota(jnp.int32, shape, 1)
+    return jnp.where(lane < shape[1] // 2, first, -first).astype(jnp.float32)
+
+
+def half_turn(array):
+    return pltpu.roll(array, array.shape[1] // 2, 1)
+
+
+def plane_kernel(field_ref, table_ref, own_ref, other_ref):
+    lanes = own_ref.shape[1]
+    result = jnp.dot(field_ref[...], table_ref[...], preferred_element_type=jnp.float32)
+    result = result.astype(jnp.bfloat16)
+    own_ref[...] = result[:, :lanes]
+    other_ref[...] = result[:, lanes:]
+
+
+def plane_call(field, table, start, count, rows):
+    step = CHANNEL_STEP
+    cells, columns = table.shape
+    lanes = columns // 2
+    shape = jax.ShapeDtypeStruct((count * rows, lanes), jnp.bfloat16)
+    out_spec = pl.BlockSpec((step * rows, lanes), lambda i: (i, 0))
+    return pl.pallas_call(
+        plane_kernel,
+        grid=(count // step,),
+        in_specs=[
+            pl.BlockSpec((step * rows, cells), lambda i: (start // step + i, 0)),
+            pl.BlockSpec((cells, columns), lambda i: (0, 0)),
+        ],
+        out_specs=[out_spec, out_spec],
+        out_shape=[shape, shape],
+        compiler_params=params(),
+        cost_estimate=cost(2 * count * rows * cells * columns, 2 * count * rows * (cells + columns)),
+        name="plane",
+    )(field, table)
+
+
+def line_kernel(rows, own_ref, recv_ref, table_ref, out_ref):
+    wide, channels, part, lanes = out_ref.shape
+    half = wide * part
+    sign = signs((half, lanes), 1.0)
+    for pair in range(0, channels, 2):
+        data = jnp.concatenate(
+            [
+                jnp.concatenate(
+                    [own_ref[c * rows : (c + 1) * rows], recv_ref[c * rows : (c + 1) * rows]], axis=0
+                )
+                for c in (pair, pair + 1)
+            ],
+            axis=1,
+        )
+        result = jnp.dot(table_ref[...], data, preferred_element_type=jnp.float32)
+        for at in range(2):
+            block = result[:, at * lanes : (at + 1) * lanes]
+            line = (block[:half] + sign * half_turn(block[half:])).astype(jnp.bfloat16)
+            for w in range(wide):
+                out_ref[w, pair + at] = line[w * part : (w + 1) * part]
+
+
+def line_call(own, recv, table, wide, rows):
+    step = CHANNEL_STEP
+    count = own.shape[0] // rows
+    lanes = own.shape[1]
+    half = table.shape[0] // 2
+    in_spec = pl.BlockSpec((step * rows, lanes), lambda i: (i, 0))
+    return pl.pallas_call(
+        functools.partial(line_kernel, rows),
+        grid=(count // step,),
+        in_specs=[in_spec, in_spec, pl.BlockSpec(table.shape, lambda i: (0, 0))],
+        out_specs=pl.BlockSpec((wide, step, half // wide, lanes), lambda i: (0, i, 0, 0)),
+        out_shape=jax.ShapeDtypeStruct((wide, count, half // wide, lanes), jnp.bfloat16),
+        compiler_params=params(),
+        cost_estimate=cost(4 * count * half * table.shape[1] * lanes, 2 * count * lanes * (half + table.shape[1])),
+        name="line",
+    )(own, recv, table)
+
+
+def spec_kernel(local_x, data_ref, table_ref, out_ref, held):
+    wide, channels, part, lanes = data_ref.shape
+    combos = part // local_x
+    kept = table_ref.shape[0] // 2
+    pairs = lanes // 2
+    sign = signs((kept, lanes), 1.0)
+    low = lax.broadcasted_iota(jnp.int32, (kept, lanes), 1) < pairs
+    for c in range(channels):
+        data = jnp.concatenate(
+            [
+                jnp.concatenate(
+                    [data_ref[w, c, j * local_x : (j + 1) * local_x] for w in range(wide)], axis=0
+                )
+                for j in range(combos)
+            ],
+            axis=1,
+        )
+        result = jnp.dot(table_ref[...], data, preferred_element_type=jnp.float32)
+        parts = []
+        for j in range(combos):
+            block = result[:, j * lanes : (j + 1) * lanes]
+            parts.append(block[:kept] + sign * half_turn(block[kept:]))
+        for j in range(0, combos - 1, 2):
+            first, second = parts[j], parts[j + 1]
+            held[:, 0, c, j * pairs : (j + 2) * pairs] = jnp.where(low, first, half_turn(second))
+            held[:, 1, c, j * pairs : (j + 2) * pairs] = jnp.where(low, half_turn(first), second)
+        if combos % 2:
+            j = combos - 1
+            held[:, 0, c, j * pairs : (j + 1) * pairs] = parts[j][:, :pairs]
+            held[:, 1, c, j * pairs : (j + 1) * pairs] = half_turn(parts[j])[:, :pairs]
+    out_ref[...] = held[...].astype(jnp.bfloat16)
+
+
+def spec_call(data, table, local_x):
+    wide, count, part, lanes = data.shape
+    step = SPEC_STEP
+    kept = table.shape[0] // 2
+    width = part // local_x * lanes // 2
+    return pl.pallas_call(
+        functools.partial(spec_kernel, local_x),
+        grid=(count // step,),
+        in_specs=[
+            pl.BlockSpec((wide, step, part, lanes), lambda i: (0, i, 0, 0)),
+            pl.BlockSpec(table.shape, lambda i: (0, 0)),
+        ],
+        out_specs=pl.BlockSpec((kept, 2, step, width), lambda i: (0, 0, i, 0)),
+        out_shape=jax.ShapeDtypeStruct((kept, 2, count, width), jnp.bfloat16),
+        scratch_shapes=[pltpu.VMEM((kept, 2, step, width), jnp.float32)],
+        compiler_params=params(),
+        cost_estimate=cost(4 * count * kept * table.shape[1] * 2 * width, 2 * data.size + 4 * kept * count * width),
+        name="spec",
+    )(data, table)
+
+
+def dual_kernel(weight_ref, grad_ref, out_ref):
+    inputs = weight_ref.shape[2]
+    grad_real = grad_ref[0, 0].astype(jnp.float32)
+    grad_imag = grad_ref[0, 1].astype(jnp.float32)
+    for i in range(0, inputs, 8):
+        real = weight_ref[0, 0, i : i + 8].astype(jnp.float32)
+        imag = weight_ref[0, 1, i : i + 8].astype(jnp.float32)
+        dual_real = jnp.sum(real * grad_real[None] + imag * grad_imag[None], axis=1)
+        dual_imag = jnp.sum(real * grad_imag[None] - imag * grad_real[None], axis=1)
+        out_ref[0, 0, i : i + 8] = dual_real.astype(jnp.bfloat16).astype(jnp.float32)
+        out_ref[0, 1, i : i + 8] = dual_imag.astype(jnp.bfloat16).astype(jnp.float32)
+
+
+def dual_call(weight, grad):
+    kept, parts, inputs, outputs, width = weight.shape
+    return pl.pallas_call(
+        dual_kernel,
+        grid=(kept,),
+        in_specs=[
+            pl.BlockSpec((1, parts, inputs, outputs, width), lambda k: (k, 0, 0, 0, 0)),
+            pl.BlockSpec((1, parts, outputs, width), lambda k: (k, 0, 0, 0)),
+        ],
+        out_specs=pl.BlockSpec((1, parts, inputs, width), lambda k: (k, 0, 0, 0)),
+        out_shape=jax.ShapeDtypeStruct((kept, parts, inputs, width), jnp.float32),
+        compiler_params=params(),
+        cost_estimate=cost(4 * weight.size, 2 * weight.size),
+        name="dual",
+    )(weight, grad)
+
+
+def outer_kernel(input_ref, grad_ref, out_ref):
+    samples = input_ref.shape[0]
+    inputs = out_ref.shape[2]
+    for i in range(0, inputs, 8):
+        real_part = 0.0
+        imag_part = 0.0
+        for n in range(samples):
+            in_real = input_ref[n, 0, 0, i : i + 8].astype(jnp.float32)[:, None, :]
+            in_imag = input_ref[n, 0, 1, i : i + 8].astype(jnp.float32)[:, None, :]
+            grad_real = grad_ref[n, 0, 0].astype(jnp.float32)[None]
+            grad_imag = grad_ref[n, 0, 1].astype(jnp.float32)[None]
+            real_part = real_part + (in_real * grad_real + in_imag * grad_imag)
+            imag_part = imag_part + (in_real * grad_imag - in_imag * grad_real)
+        out_ref[0, 0, i : i + 8] = real_part
+        out_ref[0, 1, i : i + 8] = imag_part
+
+
+def outer_call(both_input, both_grad):
+    samples, kept, parts, channels, width = both_input.shape
+    in_spec = pl.BlockSpec((samples, 1, parts, channels, width), lambda k: (0, k, 0, 0, 0))
+    out = (kept, parts, channels, channels, width)
+    return pl.pallas_call(
+        outer_kernel,
+        grid=(kept,),
+        in_specs=[in_spec, in_spec],
+        out_specs=pl.BlockSpec((1,) + out[1:], lambda k: (k, 0, 0, 0, 0)),
+        out_shape=jax.ShapeDtypeStruct(out, jnp.float32),
+        compiler_params=params(),
+        cost_estimate=cost(8 * math.prod(out), 6 * math.prod(out)),
+        name="outer",
+    )(both_input, both_grad)
+
+
+def back_x_kernel(local_x, dual_ref, table_ref, out_ref):
+    wide, channels, part, lanes = out_ref.shape
+    combos = part // local_x
+    kept = dual_ref.shape[0]
+    pairs = lanes // 2
+    cells = wide * local_x
+    sign = signs((cells, lanes), -1.0)
+    low = lax.broadcasted_iota(jnp.int32, (kept, lanes), 1) < pairs
+    for c in range(channels):
+        blocks = []
+        for j in range(0, combos - 1, 2):
+            real = dual_ref[:, 0, c, j * pairs : (j + 2) * pairs]
+            imag = dual_ref[:, 1, c, j * pairs : (j + 2) * pairs]
+            blocks.append(jnp.where(low, real, half_turn(imag)))
+            blocks.append(jnp.where(low, half_turn(real), imag))
+        if combos % 2:
+            j = combos - 1
+            real = dual_ref[:, 0, c, j * pairs : (j + 1) * pairs]
+            imag = dual_ref[:, 1, c, j * pairs : (j + 1) * pairs]
+            blocks.append(jnp.concatenate([real, imag], axis=1))
+        data = jnp.concatenate(blocks, axis=1).astype(jnp.bfloat16)
+        result = jnp.dot(table_ref[...], data, preferred_element_type=jnp.float32)
+        for j in range(combos):
+            block = result[:, j * lanes : (j + 1) * lanes]
+            back = (block[:cells] + sign * half_turn(block[cells:])).astype(jnp.bfloat16)
+            for w in range(wide):
+                out_ref[w, c, j * local_x : (j + 1) * local_x] = back[w * local_x : (w + 1) * local_x]
+
+
+def back_x_call(dual, table, wide, local_x, pairs, start, count):
+    kept, parts, channels, width = dual.shape
+    step = 8
+    part = width // pairs * local_x
+    lanes = 2 * pairs
+    return pl.pallas_call(
+        functools.partial(back_x_kernel, local_x),
+        grid=(count // step,),
+        in_specs=[
+            pl.BlockSpec((kept, parts, step, width), lambda i: (0, 0, start // step + i, 0)),
+            pl.BlockSpec(table.shape, lambda i: (0, 0)),
+        ],
+        out_specs=pl.BlockSpec((wide, step, part, lanes), lambda i: (0, i, 0, 0)),
+        out_shape=jax.ShapeDtypeStruct((wide, count, part, lanes), jnp.bfloat16),
+        compiler_params=params(),
+        cost_estimate=cost(4 * count * kept * table.shape[0] * width, 4 * kept * count * width * 2),
+        name="back_x",
+    )(dual, table)
+
+
+def back_y_kernel(rows, data_ref, table_ref, own_ref, other_ref):
+    wide, channels, part, lanes = data_ref.shape
+    half = table_ref.shape[0] // 2
+    sign = signs((half, lanes), -1.0)
+    for pair in range(0, channels, 2):
+        data = jnp.concatenate(
+            [
+                jnp.concatenate([data_ref[w, c] for w in range(wide)], axis=0)
+                for c in (pair, pair + 1)
+            ],
+            axis=1,
+        )
+        result = jnp.dot(table_ref[...], data, preferred_element_type=jnp.float32)
+        for at in range(2):
+            c = pair + at
+            block = result[:, at * lanes : (at + 1) * lanes]
+            back = (block[:half] + sign * half_turn(block[half:])).astype(jnp.bfloat16)
+            own_ref[c * rows : (c + 1) * rows] = back[:rows]
+            other_ref[c * rows : (c + 1) * rows] = back[rows:]
+
+
+def back_y_call(data, table, rows):
+    wide, count, part, lanes = data.shape
+    step = CHANNEL_STEP
+    shape = jax.ShapeDtypeStruct((count * rows, lanes), jnp.bfloat16)
+    out_spec = pl.BlockSpec((step * rows, lanes), lambda i: (i, 0))
+    return pl.pallas_call(
+        functools.partial(back_y_kernel, rows),
+        grid=(count // step,),
+        in_specs=[
+            pl.BlockSpec((wide, step, part, lanes), lambda i: (0, i, 0, 0)),
+            pl.BlockSpec(table.shape, lambda i: (0, 0)),
+        ],
+        out_specs=[out_spec, out_spec],
+        out_shape=[shape, shape],
+        compiler_params=params(),
+        cost_estimate=cost(2 * count * table.size * lanes, 2 * data.size + 4 * count * rows * lanes),
+        name="back_y",
+    )(data, table)
+
+
+def field_kernel(own_ref, recv_ref, table_ref, *out_refs):
+    data = jnp.concatenate([own_ref[...], recv_ref[...]], axis=1)
+    result = jnp.dot(data, table_ref[...], preferred_element_type=jnp.float32)
+    out_refs[-1][...] = result.astype(jnp.bfloat16)
+
+
+def field_kernel_into(own_ref, recv_ref, table_ref, so_far_ref, out_ref):
+    field_kernel(own_ref, recv_ref, table_ref, out_ref)
+
+
+def field_call(own, recv, table, total, start, rows, so_far):
+    step = CHANNEL_STEP
+    lanes = own.shape[1]
+    columns, cells = table.shape
+    count = own.shape[0] // rows
+    in_spec = pl.BlockSpec((step * rows, lanes), lambda i: (i, 0))
+    operands = [own, recv, table]
+    in_specs = [in_spec, in_spec, pl.BlockSpec((columns, cells), lambda i: (0, 0))]
+    aliases = {}
+    body = field_kernel
+    if so_far is not None:
+        operands.append(so_far)
+        in_specs.append(pl.BlockSpec(memory_space=pl.ANY))
+        aliases = {3: 0}
+        body = field_kernel_into
+    return pl.pallas_call(
+        body,
+        grid=(count // step,),
+        in_specs=in_specs,
+        out_specs=pl.BlockSpec((step * rows, cells), lambda i: (start // step + i, 0)),
+        out_shape=jax.ShapeDtypeStruct((total * rows, cells), jnp.bfloat16),
+        input_output_aliases=aliases,
+        compiler_params=params(),
+        cost_estimate=cost(2 * count * rows * columns * cells, 2 * count * rows * (columns + cells)),
+        name="field",
+    )(*operands)
+
+
+def fast_shards(layer_input, output_cotangent, spectral_weight):
+    channels, local_x, local_y, cells = layer_input.shape[1:]
+    wide = lax.axis_size("wide")
+    rows = local_x * local_y
+    me = lax.axis_index("narrow")
+    swap = [(0, 1), (1, 0)]
+    orders = ((0, 1), (1, 0))
+    plain, doubled, inverse = zip(*(zt_tables(list(order)) for order in orders))
+    forward_y, back_y = zip(*(y_tables(order, local_y, local_x) for order in orders))
+    plain, doubled, inverse = pick(plain, me), pick(doubled, me), pick(inverse, me)
+    forward_y, back_y = pick(forward_y, me), pick(back_y, me)
+    forward_x, back_x = (jnp.asarray(table) for table in x_tables())
+    pairs = plain.shape[1] // 4
+
+    def flat(field):
+        return jnp.transpose(field[0], (0, 2, 1, 3)).reshape(channels * rows, cells)
+
+    def to_modes(field, table, chunks):
+        count = channels // chunks
+        outs = []
+        for start in range(0, channels, count):
+            own, other = plane_call(field, table, start, count, rows)
+            recv = lax.ppermute(other, "narrow", swap)
+            line = line_call(own, recv, forward_y, wide, rows)
+            line = lax.all_to_all(line, "wide", split_axis=0, concat_axis=0, tiled=True)
+            outs.append(spec_call(line, forward_x, local_x))
+        return outs[0] if chunks == 1 else jnp.concatenate(outs, axis=2)
+
+    grad_spec = to_modes(flat(output_cotangent), doubled, GRAD_CHUNKS)
+    input_spec = to_modes(flat(layer_input), plain, INPUT_CHUNKS)
+    kept = grad_spec.shape[0]
+    weight = jnp.transpose(spectral_weight[0], (1, 2, 3, 4, 0))
+    dual = dual_call(weight, grad_spec)
+
+    def both(spec):
+        n_rep = lax.axis_size("rep")
+        halves = spec.reshape((n_rep, kept // n_rep) + spec.shape[1:])
+        return lax.all_to_all(halves, "rep", split_axis=0, concat_axis=0, tiled=True)
+
+    weight_grad = outer_call(both(input_spec), both(grad_spec))
+    weight_grad = jnp.transpose(weight_grad, (4, 0, 1, 2, 3))
+
+    count = channels // BACK_CHUNKS
+    result = None
+    for start in range(0, channels, count):
+        block = back_x_call(dual, back_x, wide, local_x, pairs, start, count)
+        block = lax.all_to_all(block, "wide", split_axis=0, concat_axis=0, tiled=True)
+        own, other = back_y_call(block, back_y, rows)
+        recv = lax.ppermute(other, "narrow", swap)
+        result = field_call(own, recv, inverse, channels, start, rows, result)
+    field = result.reshape(channels, local_y, local_x, cells)
+    return (jnp.transpose(field, (0, 2, 1, 3))[None], weight_grad[None])
+
+
+def aligned(mesh):
+    wide, narrow = mesh.shape["wide"], mesh.shape["narrow"]
+    return narrow == 2 and (2 * MY) % wide == 0 and (NX // wide) % 16 == 0 and NY % narrow == 0
+
+
 def solution(mesh):
     in_specs = (
         P("rep", None, "wide", "narrow", None),
@@ -175,4 +640,5 @@
         P("rep", None, "wide", "narrow", None),
         P("narrow", "wide", "rep", None, None, None),
     )
-    return jax.shard_map(shards, mesh=mesh, in_specs=in_specs, out_specs=out_specs, check_vma=False)
+    body = fast_shards if aligned(mesh) else shards
+    return jax.shard_map(body, mesh=mesh, in_specs=in_specs, out_specs=out_specs, check_vma=False)

time: 1030 us -> 407 us (0.40); the launches traced: 1010 us -> 405 us
  local copies, waits for them, and re-layouts: 747 us -> 9.97 us
  waiting for transfers between devices: 51.6 us -> 176 us
  Pallas kernels: 0 us -> 117 us
  other arithmetic: 92.1 us -> 0 us
  blocking collectives: 0 us -> 81.6 us
  matrix products: 69.8 us -> 0 us
  starting transfers between devices: 37 us -> 20.4 us
  between operations: 14.9 us -> 0.76 us
    unnamed x43 -> x24, local copies, waits for them, and re-layouts: 281 us -> 6.59 us
    all_to_all x8 -> x0, local copies, waits for them, and re-layouts: 159 us -> none  [the longest x2 49.2 us: shards(): lax.all_to_all(grad_plane, 'narrow', split_axis=4, concat_axis=2, tiled=T...]
    reshape x8 -> x0, local copies, waits for them, and re-layouts: 155 us -> none  [the longest x2 46.5 us: shards(): grad_plane.astype(jnp.bfloat16)]
    ppermute x0 -> x3, waiting for transfers between devices: none -> 124 us  [the longest x2 124 us: to_modes(): recv = lax.ppermute(other, 'narrow', swap)]
    pallas_call x0 -> x11, Pallas kernels: none -> 117 us  [the longest x2 27.5 us: plane_call(): pl.pallas_call(plane_kernel, grid=(count // step,), in_specs=[pl.BlockSpe...]
    another operation x3 -> x0, local copies, waits for them, and re-layouts: 98.8 us -> none  [the longest x1 33 us: shards(): grad_field.reshape(-1, plane_cells)]
    all_to_all x0 -> x2, blocking collectives: none -> 81.6 us  [the longest x1 76.2 us: to_modes(): line = lax.all_to_all(line, 'wide', split_axis=0, concat_axis=0, tiled=True)]
    dot_general x9 -> x0, matrix products: 69.8 us -> none  [the longest x1 14.3 us: shards(): jnp.dot(block_part.reshape(-1, 2 * pair_count), inverse, preferred_elemen...]
  transfers between devices with their start and end apart: 8 -> 6, of which waited for: 4 -> 3; matrix products, arithmetic and copies ran while one was open for 55% -> 1% of each run, Pallas kernels for 0% -> 12%
where the time goes in v1:
time: 407 us; the launch traced here: 405 us
  waiting for transfers between devices  176 us (43%)
  Pallas kernels  117 us (29%)
  blocking collectives  81.6 us (20%)
  starting transfers between devices  20.4 us (5%)
  local copies, waits for them, and re-layouts  9.97 us (2%)
    ppermute x2, waiting for transfers between devices, to_modes(): recv = lax.ppermute(other, 'narrow', swap)  124 us
    all_to_all x1, blocking collectives, to_modes(): line = lax.all_to_all(line, 'wide', split_axis=0, concat_axis=0, tiled=True)  76.2 us
    all_to_all x1, waiting for transfers between devices, to_modes(): line = lax.all_to_all(line, 'wide', split_axis=0, concat_axis=0, tiled=True)  51.5 us
    pallas_call x2, Pallas kernels, plane_call(): pl.pallas_call(plane_kernel, grid=(count // step,), in_specs=[pl.BlockSpe...  27.5 us
    pallas_call x1, Pallas kernels, dual_call(): pl.pallas_call(dual_kernel, grid=(kept,), in_specs=[pl.BlockSpec((1, part...  23.7 us
    pallas_call x2, Pallas kernels, line_call(): pl.pallas_call(functools.partial(line_kernel, rows), grid=(count // step,...  20 us
    pallas_call x1, Pallas kernels, outer_call(): pl.pallas_call(outer_kernel, grid=(kept,), in_specs=[in_spec, in_spec], o...  13.3 us
    pallas_call x1, Pallas kernels, field_call(): pl.pallas_call(body, grid=(count // step,), in_specs=in_specs, out_specs=...  12.2 us
  transfers between devices with their start and end apart: 6, of which 3 were waited for; matrix products, arithmetic and copies ran while one was open for 1% of the time, Pallas kernels for 12%

profile of v1, /device:TPU:0, one launch (start us, length us, event | category | flops | bytes accessed | tf_op | source)
XLA Modules:
  0.0 405.1 jit_solution(15050386346315906761)
XLA Ops:
  0.6 1.1 dynamic-slice_bitcast_fusion.4.table_ref
  1.7 0.0 copy-start.7
  1.7 13.8 %plane.2 = (bf16[11264,128]{1,0:T(8,128)(2,1)S(1)}, bf16[11264,128]{1,0:T(8,128)(2,1)}) custom-call(bf16[11264,1024]{1,0:T(8,128)(2,1)} %bitcast.37, bf16[1024,256]{1,0:T(8,128)(2,1)S(1)} %dynamic-slice_bitcast_fusion.4.table_ref), custom_call_target="tpu_custom_call" | custom-call | flops 5905580032 | bytes 28835840 | tf_op jit(solution)/shard_map/plane/pallas_call | solution.py:274
  15.5 2.9 collective-permute-start
  18.5 0.0 copy-done.7
  18.5 0.1 dynamic-slice_bitcast_fusion.table_ref
  18.6 62.6 %collective-permute-done.recv_ref = bf16[11264,128]{1,0:T(8,128)(2,1)S(1)} collective-permute-done((bf16[11264,128]{1,0:T(8,128)(2,1)}, bf16[11264,128]{1,0:T(8,128)(2,1)S(1)}, u32[]{:S(2)}, u32[]{:S(2)}) %collective-permute-start) | collective-permute-done | bytes 2883616 | tf_op jit(solution)/shard_map/ppermute | solution.py:596
  81.2 0.0 copy-start.10
  81.2 1.6 copy-done.10
  82.7 10.0 %line.2 = bf16[8,32,48,128]{3,2,1,0:T(8,128)(2,1)} custom-call(bf16[11264,128]{1,0:T(8,128)(2,1)S(1)} %get-tuple-element.8.own_ref, bf16[11264,128]{1,0:T(8,128)(2,1)} %copy-done.10, bf16[768,704]{1,0:T(8,128)(2,1)S(1)} %dynamic-slice_bitcast_fusion.table_ref), custom_call_target="tpu_custom_call" | custom-call | flops 4429185024 | bytes 8912896 | tf_op jit(solution)/shard_map/line/pallas_call | solution.py:317
  92.8 0.0 copy-start.6
  92.8 76.2 %all_to_all.25.data_ref = bf16[8,32,48,128]{3,2,1,0:T(8,128)(2,1)S(1)} all-to-all(bf16[8,32,48,128]{3,2,1,0:T(8,128)(2,1)} %line.2), channel_id=1, replica_groups=mesh['wide'=8,'narrow'=2,'rep'=2] {'wide'}, dimensions={0} | all-to-all | bytes 6291456 | tf_op jit(solution)/shard_map/all_to_all | solution.py:598
  168.9 0.0 copy-done.6
  168.9 2.2 spec.2.grad_ref
  171.2 0.0 copy-start.5
  171.2 23.7 %dual.1.dual_ref = f32[24,2,32,192]{3,2,1,0:T(8,128)S(1)} custom-call(bf16[24,2,32,32,192]{4,3,2,1,0:T(8,128)(2,1)} %bitcast.36, bf16[24,2,32,192]{3,2,1,0:T(8,128)(2,1)S(1)} %spec.2.grad_ref), custom_call_target="tpu_custom_call" | custom-call | flops 37748736 | bytes 18874368 | tf_op jit(solution)/shard_map/dual/pallas_call | solution.py:398
  194.9 0.0 copy-start
  194.9 0.9 copy-done
  195.8 0.0 copy-done.5
  195.8 4.1 %back_x.1 = bf16[8,32,48,128]{3,2,1,0:T(8,128)(2,1)} custom-call(f32[24,2,32,192]{3,2,1,0:T(8,128)S(1)} %dual.1.dual_ref, bf16[256,24]{1,0:T(8,128)(2,1)S(1)} %copy-done.5), custom_call_target="tpu_custom_call" | custom-call | flops 150994944 | bytes 1179648 | tf_op jit(solution)/shard_map/back_x/pallas_call | solution.py:480
  199.9 4.6 %all-to-all-start.1 = ((bf16[8,32,48,128]{3,2,1,0:T(8,128)(2,1)}), bf16[8,32,48,128]{3,2,1,0:T(8,128)(2,1)}, u32[]{:S(2)}, u32[]{:S(2)}) async-start(bf16[8,32,48,128]{3,2,1,0:T(8,128)(2,1)} %back_x.1), calls=%async_computation.1 | async-start | bytes 6291456 | tf_op jit(solution)/shard_map/all_to_all | solution.py:620
  204.5 0.0 copy-done.9
  204.6 13.7 %plane.3 = (bf16[11264,128]{1,0:T(8,128)(2,1)S(1)}, bf16[11264,128]{1,0:T(8,128)(2,1)}) custom-call(bf16[11264,1024]{1,0:T(8,128)(2,1)} %bitcast.38, bf16[1024,256]{1,0:T(8,128)(2,1)S(1)} %dynamic-slice_bitcast_fusion.2.table_ref), custom_call_target="tpu_custom_call" | custom-call | flops 5905580032 | bytes 28835840 | tf_op jit(solution)/shard_map/plane/pallas_call | solution.py:274
  218.2 1.5 collective-permute-start.2
  219.7 61.6 %collective-permute-done.2.recv_ref = bf16[11264,128]{1,0:T(8,128)(2,1)S(1)} collective-permute-done((bf16[11264,128]{1,0:T(8,128)(2,1)}, bf16[11264,128]{1,0:T(8,128)(2,1)S(1)}, u32[]{:S(2)}, u32[]{:S(2)}) %collective-permute-start.2) | collective-permute-done | bytes 2883616 | tf_op jit(solution)/shard_map/ppermute | solution.py:596
  281.3 1.6 copy-done.11
  282.9 10.0 %line.3 = bf16[8,32,48,128]{3,2,1,0:T(8,128)(2,1)} custom-call(bf16[11264,128]{1,0:T(8,128)(2,1)S(1)} %get-tuple-element.12.own_ref, bf16[11264,128]{1,0:T(8,128)(2,1)} %copy-done.11, bf16[768,704]{1,0:T(8,128)(2,1)S(1)} %dynamic-slice_bitcast_fusion.table_ref), custom_call_target="tpu_custom_call" | custom-call | flops 4429185024 | bytes 8912896 | tf_op jit(solution)/shard_map/line/pallas_call | solution.py:317
  292.9 0.0 all-to-all-done.1.data_ref
  292.9 5.6 %all-to-all-start.2 = ((bf16[8,32,48,128]{3,2,1,0:T(8,128)(2,1)}), bf16[8,32,48,128]{3,2,1,0:T(8,128)(2,1)S(1)}, u32[]{:S(2)}, u32[]{:S(2)}) async-start(bf16[8,32,48,128]{3,2,1,0:T(8,128)(2,1)} %line.3), calls=%async_computation.2 | async-start | bytes 6291456 | tf_op jit(solution)/shard_map/all_to_all | solution.py:598
  298.5 1.3 dynamic-slice_bitcast_fusion.1.table_ref
  299.9 0.0 copy-start.8
  299.9 11.3 %back_y.1 = (bf16[11264,128]{1,0:T(8,128)(2,1)S(1)}, bf16[11264,128]{1,0:T(8,128)(2,1)}) custom-call(bf16[8,32,48,128]{3,2,1,0:T(8,128)(2,1)} %all-to-all-done.1.data_ref, bf16[1408,384]{1,0:T(8,128)(2,1)S(1)} %dynamic-slice_bitcast_fusion.1.table_ref), custom_call_target="tpu_custom_call" | custom-call | flops 4429185024 | bytes 8912896 | tf_op jit(solution)/shard_map/back_y/pallas_call | solution.py:521
  311.2 1.6 copy-done.2
  312.8 1.5 collective-permute-start.1
  314.3 0.0 copy-done.8
  314.3 0.8 dynamic-slice_bitcast_fusion.3.table_ref
  315.1 51.5 %all-to-all-done.2.data_ref = bf16[8,32,48,128]{3,2,1,0:T(8,128)(2,1)S(1)} async-done(((bf16[8,32,48,128]{3,2,1,0:T(8,128)(2,1)}), bf16[8,32,48,128]{3,2,1,0:T(8,128)(2,1)S(1)}, u32[]{:S(2)}, u32[]{:S(2)}) %all-to-all-start.2) | async-done | bytes 3145760 | tf_op jit(solution)/shard_map/all_to_all | solution.py:598
  366.7 4.3 %all-to-all-start.4 = ((bf16[2,12,2,32,192]{4,3,2,1,0:T(8,128)(2,1)}), bf16[2,12,2,32,192]{4,3,2,1,0:T(8,128)(2,1)}, u32[]{:S(2)}, u32[]{:S(2)}) async-start(bf16[2,12,2,32,192]{4,3,2,1,0:T(8,128)(2,1)} %bitcast.33), calls=%async_computation.4 | async-start | bytes 1572864 | tf_op jit(solution)/shard_map/all_to_all | solution.py:611
  371.0 2.2 spec.3
  373.2 0.0 copy-start.1
  373.2 0.9 copy-done.1
  374.1 0.0 all-to-all-done.4.grad_ref
  374.1 5.5 %all_to_all.26.input_ref = bf16[2,12,2,32,192]{4,3,2,1,0:T(8,128)(2,1)S(1)} all-to-all(bf16[2,12,2,32,192]{4,3,2,1,0:T(8,128)(2,1)} %bitcast.34), channel_id=1, replica_groups=mesh['wide'=8,'narrow'=2,'rep'=2] {'rep'}, dimensions={0} | all-to-all | bytes 1179648 | tf_op jit(solution)/shard_map/all_to_all | solution.py:611
  379.6 13.3 %outer.1 = f32[12,2,32,32,192]{4,3,2,1,0:T(8,128)} custom-call(bf16[2,12,2,32,192]{4,3,2,1,0:T(8,128)(2,1)S(1)} %all_to_all.26.input_ref, bf16[2,12,2,32,192]{4,3,2,1,0:T(8,128)(2,1)} %all-to-all-done.4.grad_ref), custom_call_target="tpu_custom_call" | custom-call | flops 37748736 | bytes 28311552 | tf_op jit(solution)/shard_map/outer/pallas_call | solution.py:434
  392.9 0.0 collective-permute-done.1.recv_ref
  392.9 0.0 copy-done.3
  392.9 0.0 copy-done.4
  392.9 12.2 %field.1 = bf16[11264,1024]{1,0:T(8,128)(2,1)} custom-call(bf16[11264,128]{1,0:T(8,128)(2,1)S(1)} %copy-done.3, bf16[11264,128]{1,0:T(8,128)(2,1)} %collective-permute-done.1.recv_ref, bf16[256,1024]{1,0:T(8,128)(2,1)S(1)} %copy-done.4), custom_call_target="tpu_custom_call" | custom-call | flops 5905580032 | bytes 28835840 | tf_op jit(solution)/shard_map/field/pallas_call | solution.py:561
  (6 shorter events, 0.1 us)
Async XLA Ops:
  1.7 16.8 %copy-start.7 = (bf16[2,768,704]{2,1,0:T(8,128)(2,1)S(1)}, bf16[2,768,704]{2,1,0:T(8,128)(2,1)}, u32[]{:S(2)}) copy-start(bf16[2,768,704]{2,1,0:T(8,128)(2,1)} %constant.41.clone) | copy-start | bytes 6488068
  15.5 65.6 %collective-permute-start = (bf16[11264,128]{1,0:T(8,128)(2,1)}, bf16[11264,128]{1,0:T(8,128)(2,1)S(1)}, u32[]{:S(2)}, u32[]{:S(2)}) collective-permute-start(bf16[11264,128]{1,0:T(8,128)(2,1)} %get-tuple-element.9), channel_id=1, source_target_pairs={{0,2},{2,0},{1,3},{3,1},{4,6},{6,4},{5,7},{7,5},{8,10},{10,8},{9,1... | collective-permute-start | bytes 8650760 | tf_op jit(solution)/shard_map/ppermute | solution.py:596
  81.2 1.6 copy-start.10
  92.8 76.2 %copy-start.6 = (bf16[48,128]{1,0:T(8,128)(2,1)S(1)}, bf16[48,128]{1,0:T(8,128)(2,1)}, u32[]{:S(2)}) copy-start(bf16[48,128]{1,0:T(8,128)(2,1)} %constant.43.clone.table_ref) | copy-start | bytes 36868
  171.2 24.6 %copy-start.5 = (bf16[256,24]{1,0:T(8,128)(2,1)S(1)}, bf16[256,24]{1,0:T(8,128)(2,1)}, u32[]{:S(2)}) copy-start(bf16[256,24]{1,0:T(8,128)(2,1)} %constant.44.clone.table_ref) | copy-start | bytes 36868
  194.9 0.9 copy-start
  199.9 4.6 %copy-start.9 = (bf16[2,1024,256]{2,1,0:T(8,128)(2,1)S(1)}, bf16[2,1024,256]{2,1,0:T(8,128)(2,1)}, u32[]{:S(2)}) copy-start(bf16[2,1024,256]{2,1,0:T(8,128)(2,1)} %constant.38.clone) | copy-start | bytes 3145732
  199.9 93.0 %all-to-all-start.1 = ((bf16[8,32,48,128]{3,2,1,0:T(8,128)(2,1)}), bf16[8,32,48,128]{3,2,1,0:T(8,128)(2,1)}, u32[]{:S(2)}, u32[]{:S(2)}) async-start(bf16[8,32,48,128]{3,2,1,0:T(8,128)(2,1)} %back_x.1), calls=%async_computation.1 | async-start | bytes 6291456 | tf_op jit(solution)/shard_map/all_to_all | solution.py:620
  218.2 63.1 %collective-permute-start.2 = (bf16[11264,128]{1,0:T(8,128)(2,1)}, bf16[11264,128]{1,0:T(8,128)(2,1)S(1)}, u32[]{:S(2)}, u32[]{:S(2)}) collective-permute-start(bf16[11264,128]{1,0:T(8,128)(2,1)} %get-tuple-element.13), channel_id=1, source_target_pairs={{0,2},{2,0},{1,3},{3,1},{4,6},{6,4},{5,7},{7,5},{8,10},{10,8},{9,1... | collective-permute-start | bytes 8650760 | tf_op jit(solution)/shard_map/ppermute | solution.py:596
  281.3 1.6 copy-start.11
  292.9 73.8 %all-to-all-start.2 = ((bf16[8,32,48,128]{3,2,1,0:T(8,128)(2,1)}), bf16[8,32,48,128]{3,2,1,0:T(8,128)(2,1)S(1)}, u32[]{:S(2)}, u32[]{:S(2)}) async-start(bf16[8,32,48,128]{3,2,1,0:T(8,128)(2,1)} %line.3), calls=%async_computation.2 | async-start | bytes 6291456 | tf_op jit(solution)/shard_map/all_to_all | solution.py:598
  299.9 14.4 %copy-start.8 = (bf16[2,256,1024]{2,1,0:T(8,128)(2,1)S(1)}, bf16[2,256,1024]{2,1,0:T(8,128)(2,1)}, u32[]{:S(2)}) copy-start(bf16[2,256,1024]{2,1,0:T(8,128)(2,1)} %constant.40.clone) | copy-start | bytes 3145732
  311.2 1.6 copy-start.2
  312.8 80.0 %collective-permute-start.1 = (bf16[11264,128]{1,0:T(8,128)(2,1)}, bf16[11264,128]{1,0:T(8,128)(2,1)}, u32[]{:S(2)}, u32[]{:S(2)}) collective-permute-start(bf16[11264,128]{1,0:T(8,128)(2,1)} %get-tuple-element.11), channel_id=1, source_target_pairs={{0,2},{2,0},{1,3},{3,1},{4,6},{6,4},{5,7},{7,5},{8,10},{10,8},{9,1... | collective-permute-start | bytes 8650760 | tf_op jit(solution)/shard_map/ppermute | solution.py:622
  366.7 7.4 %all-to-all-start.4 = ((bf16[2,12,2,32,192]{4,3,2,1,0:T(8,128)(2,1)}), bf16[2,12,2,32,192]{4,3,2,1,0:T(8,128)(2,1)}, u32[]{:S(2)}, u32[]{:S(2)}) async-start(bf16[2,12,2,32,192]{4,3,2,1,0:T(8,128)(2,1)} %bitcast.33), calls=%async_computation.4 | async-start | bytes 1572864 | tf_op jit(solution)/shard_map/all_to_all | solution.py:611
  373.2 0.9 copy-start.1
  379.6 13.3 %copy-start.3 = (bf16[11264,128]{1,0:T(8,128)(2,1)S(1)}, bf16[11264,128]{1,0:T(8,128)(2,1)}, u32[]{:S(2)}) copy-start(bf16[11264,128]{1,0:T(8,128)(2,1)} %copy-done.2) | copy-start | bytes 8650756
  379.6 13.3 %copy-start.4 = (bf16[256,1024]{1,0:T(8,128)(2,1)S(1)}, bf16[256,1024]{1,0:T(8,128)(2,1)}, u32[]{:S(2)}) copy-start(bf16[256,1024]{1,0:T(8,128)(2,1)} %dynamic-slice_bitcast_fusion.3.table_ref) | copy-start | bytes 1572868

commit v2 on v1

--- a/solution.py
+++ b/solution.py
@@ -20,10 +20,7 @@
 NT = 16
 
 CHANNEL_STEP = 4
-SPEC_STEP = 16
-GRAD_CHUNKS = 1
-INPUT_CHUNKS = 1
-BACK_CHUNKS = 1
+CHUNKS = 2
 VMEM_BYTES = 48 * 1024 * 1024
 
 
@@ -248,6 +245,18 @@
     return pl.CostEstimate(flops=int(flops), bytes_accessed=int(moved), transcendentals=0)
 
 
+def call(body, operands, in_specs, after, **settings):
+    held_back = len(operands)
+    if after is None:
+        return pl.pallas_call(body, in_specs=in_specs, **settings)(*operands)
+
+    def without(*refs):
+        body(*refs[:held_back], *refs[held_back + 1 :])
+
+    specs = list(in_specs) + [pl.BlockSpec(memory_space=pl.ANY)]
+    return pl.pallas_call(without, in_specs=specs, **settings)(*operands, after)
+
+
 def signs(shape, first):
     lane = lax.broadcasted_iota(jnp.int32, shape, 1)
     return jnp.where(lane < shape[1] // 2, first, -first).astype(jnp.float32)
@@ -265,25 +274,27 @@
     other_ref[...] = result[:, lanes:]
 
 
-def plane_call(field, table, start, count, rows):
+def plane_call(field, table, start, count, rows, after=None):
     step = CHANNEL_STEP
     cells, columns = table.shape
     lanes = columns // 2
     shape = jax.ShapeDtypeStruct((count * rows, lanes), jnp.bfloat16)
     out_spec = pl.BlockSpec((step * rows, lanes), lambda i: (i, 0))
-    return pl.pallas_call(
+    return call(
         plane_kernel,
-        grid=(count // step,),
-        in_specs=[
+        [field, table],
+        [
             pl.BlockSpec((step * rows, cells), lambda i: (start // step + i, 0)),
             pl.BlockSpec((cells, columns), lambda i: (0, 0)),
         ],
+        after,
+        grid=(count // step,),
         out_specs=[out_spec, out_spec],
         out_shape=[shape, shape],
         compiler_params=params(),
         cost_estimate=cost(2 * count * rows * cells * columns, 2 * count * rows * (cells + columns)),
         name="plane",
-    )(field, table)
+    )
 
 
 def line_kernel(rows, own_ref, recv_ref, table_ref, out_ref):
@@ -308,36 +319,40 @@
                 out_ref[w, pair + at] = line[w * part : (w + 1) * part]
 
 
-def line_call(own, recv, table, wide, rows):
+def line_call(own, recv, table, wide, rows, after=None):
     step = CHANNEL_STEP
     count = own.shape[0] // rows
     lanes = own.shape[1]
     half = table.shape[0] // 2
     in_spec = pl.BlockSpec((step * rows, lanes), lambda i: (i, 0))
-    return pl.pallas_call(
+    return call(
         functools.partial(line_kernel, rows),
+        [own, recv, table],
+        [in_spec, in_spec, pl.BlockSpec(table.shape, lambda i: (0, 0))],
+        after,
         grid=(count // step,),
-        in_specs=[in_spec, in_spec, pl.BlockSpec(table.shape, lambda i: (0, 0))],
         out_specs=pl.BlockSpec((wide, step, half // wide, lanes), lambda i: (0, i, 0, 0)),
         out_shape=jax.ShapeDtypeStruct((wide, count, half // wide, lanes), jnp.bfloat16),
         compiler_params=params(),
         cost_estimate=cost(4 * count * half * table.shape[1] * lanes, 2 * count * lanes * (half + table.shape[1])),
         name="line",
-    )(own, recv, table)
-
-
-def spec_kernel(local_x, data_ref, table_ref, out_ref, held):
-    wide, channels, part, lanes = data_ref.shape
+    )
+
+
+def spec_kernel(local_x, *refs):
+    *data_refs, table_ref, out_ref, held = refs
+    wide, channels, part, lanes = data_refs[0].shape
     combos = part // local_x
     kept = table_ref.shape[0] // 2
     pairs = lanes // 2
     sign = signs((kept, lanes), 1.0)
     low = lax.broadcasted_iota(jnp.int32, (kept, lanes), 1) < pairs
-    for c in range(channels):
+    for c in range(len(data_refs) * channels):
+        data_ref = data_refs[c // channels]
         data = jnp.concatenate(
             [
                 jnp.concatenate(
-                    [data_ref[w, c, j * local_x : (j + 1) * local_x] for w in range(wide)], axis=0
+                    [data_ref[w, c % channels, j * local_x : (j + 1) * local_x] for w in range(wide)], axis=0
                 )
                 for j in range(combos)
             ],
@@ -359,28 +374,31 @@
     out_ref[...] = held[...].astype(jnp.bfloat16)
 
 
-def spec_call(data, table, local_x):
-    wide, count, part, lanes = data.shape
-    step = SPEC_STEP
+def spec_call(chunks, table, local_x, after=None):
+    wide, step, part, lanes = chunks[0].shape
+    count = len(chunks) * step
     kept = table.shape[0] // 2
     width = part // local_x * lanes // 2
-    return pl.pallas_call(
+    whole = pl.BlockSpec((wide, step, part, lanes), lambda i: (0, 0, 0, 0))
+    return call(
         functools.partial(spec_kernel, local_x),
-        grid=(count // step,),
-        in_specs=[
-            pl.BlockSpec((wide, step, part, lanes), lambda i: (0, i, 0, 0)),
-            pl.BlockSpec(table.shape, lambda i: (0, 0)),
-        ],
-        out_specs=pl.BlockSpec((kept, 2, step, width), lambda i: (0, 0, i, 0)),
+        [*chunks, table],
+        [whole] * len(chunks) + [pl.BlockSpec(table.shape, lambda i: (0, 0))],
+        after,
+        grid=(1,),
+        out_specs=pl.BlockSpec((kept, 2, count, width), lambda i: (0, 0, 0, 0)),
         out_shape=jax.ShapeDtypeStruct((kept, 2, count, width), jnp.bfloat16),
-        scratch_shapes=[pltpu.VMEM((kept, 2, step, width), jnp.float32)],
+        scratch_shapes=[pltpu.VMEM((kept, 2, count, width), jnp.float32)],
         compiler_params=params(),
-        cost_estimate=cost(4 * count * kept * table.shape[1] * 2 * width, 2 * data.size + 4 * kept * count * width),
+        cost_estimate=cost(
+            4 * count * kept * table.shape[1] * 2 * width, 2 * wide * count * part * lanes
+        ),
         name="spec",
-    )(data, table)
-
-
-def dual_kernel(weight_ref, grad_ref, out_ref):
+    )
+
+
+def dual_kernel(last, weight_ref, grad_ref, *refs):
+    out_ref = refs[-1]
     inputs = weight_ref.shape[2]
     grad_real = grad_ref[0, 0].astype(jnp.float32)
     grad_imag = grad_ref[0, 1].astype(jnp.float32)
@@ -389,25 +407,38 @@
         imag = weight_ref[0, 1, i : i + 8].astype(jnp.float32)
         dual_real = jnp.sum(real * grad_real[None] + imag * grad_imag[None], axis=1)
         dual_imag = jnp.sum(real * grad_imag[None] - imag * grad_real[None], axis=1)
-        out_ref[0, 0, i : i + 8] = dual_real.astype(jnp.bfloat16).astype(jnp.float32)
-        out_ref[0, 1, i : i + 8] = dual_imag.astype(jnp.bfloat16).astype(jnp.float32)
-
-
-def dual_call(weight, grad):
-    kept, parts, inputs, outputs, width = weight.shape
-    return pl.pallas_call(
-        dual_kernel,
+        for s, part in enumerate((dual_real, dual_imag)):
+            if len(refs) > 1:
+                part = part + refs[0][0, s, i : i + 8]
+            if last:
+                part = part.astype(jnp.bfloat16).astype(jnp.float32)
+            out_ref[0, s, i : i + 8] = part
+
+
+def dual_call(weight, grad, start, so_far, last, after=None):
+    kept, parts, inputs, _, width = weight.shape
+    count = grad.shape[2]
+    out_spec = pl.BlockSpec((1, parts, inputs, width), lambda k: (k, 0, 0, 0))
+    operands = [weight, grad]
+    in_specs = [
+        pl.BlockSpec((1, parts, inputs, count, width), lambda k: (k, 0, 0, start // count, 0)),
+        pl.BlockSpec((1, parts, count, width), lambda k: (k, 0, 0, 0)),
+    ]
+    if so_far is not None:
+        operands.append(so_far)
+        in_specs.append(out_spec)
+    return call(
+        functools.partial(dual_kernel, last),
+        operands,
+        in_specs,
+        after,
         grid=(kept,),
-        in_specs=[
-            pl.BlockSpec((1, parts, inputs, outputs, width), lambda k: (k, 0, 0, 0, 0)),
-            pl.BlockSpec((1, parts, outputs, width), lambda k: (k, 0, 0, 0)),
-        ],
-        out_specs=pl.BlockSpec((1, parts, inputs, width), lambda k: (k, 0, 0, 0)),
+        out_specs=out_spec,
         out_shape=jax.ShapeDtypeStruct((kept, parts, inputs, width), jnp.float32),
         compiler_params=params(),
-        cost_estimate=cost(4 * weight.size, 2 * weight.size),
+        cost_estimate=cost(4 * kept * inputs * count * width, 4 * kept * inputs * count * width),
         name="dual",
-    )(weight, grad)
+    )
 
 
 def outer_kernel(input_ref, grad_ref, out_ref):
@@ -427,20 +458,22 @@
         out_ref[0, 1, i : i + 8] = imag_part
 
 
-def outer_call(both_input, both_grad):
+def outer_call(both_input, both_grad, after=None):
     samples, kept, parts, channels, width = both_input.shape
     in_spec = pl.BlockSpec((samples, 1, parts, channels, width), lambda k: (0, k, 0, 0, 0))
     out = (kept, parts, channels, channels, width)
-    return pl.pallas_call(
+    return call(
         outer_kernel,
+        [both_input, both_grad],
+        [in_spec, in_spec],
+        after,
         grid=(kept,),
-        in_specs=[in_spec, in_spec],
         out_specs=pl.BlockSpec((1,) + out[1:], lambda k: (k, 0, 0, 0, 0)),
         out_shape=jax.ShapeDtypeStruct(out, jnp.float32),
         compiler_params=params(),
         cost_estimate=cost(8 * math.prod(out), 6 * math.prod(out)),
         name="outer",
-    )(both_input, both_grad)
+    )
 
 
 def back_x_kernel(local_x, dual_ref, table_ref, out_ref):
@@ -472,24 +505,26 @@
                 out_ref[w, c, j * local_x : (j + 1) * local_x] = back[w * local_x : (w + 1) * local_x]
 
 
-def back_x_call(dual, table, wide, local_x, pairs, start, count):
+def back_x_call(dual, table, wide, local_x, pairs, start, count, after=None):
     kept, parts, channels, width = dual.shape
     step = 8
     part = width // pairs * local_x
     lanes = 2 * pairs
-    return pl.pallas_call(
+    return call(
         functools.partial(back_x_kernel, local_x),
-        grid=(count // step,),
-        in_specs=[
+        [dual, table],
+        [
             pl.BlockSpec((kept, parts, step, width), lambda i: (0, 0, start // step + i, 0)),
             pl.BlockSpec(table.shape, lambda i: (0, 0)),
         ],
+        after,
+        grid=(count // step,),
         out_specs=pl.BlockSpec((wide, step, part, lanes), lambda i: (0, i, 0, 0)),
         out_shape=jax.ShapeDtypeStruct((wide, count, part, lanes), jnp.bfloat16),
         compiler_params=params(),
         cost_estimate=cost(4 * count * kept * table.shape[0] * width, 4 * kept * count * width * 2),
         name="back_x",
-    )(dual, table)
+    )
 
 
 def back_y_kernel(rows, data_ref, table_ref, own_ref, other_ref):
@@ -513,24 +548,26 @@
             other_ref[c * rows : (c + 1) * rows] = back[rows:]
 
 
-def back_y_call(data, table, rows):
+def back_y_call(data, table, rows, after=None):
     wide, count, part, lanes = data.shape
     step = CHANNEL_STEP
     shape = jax.ShapeDtypeStruct((count * rows, lanes), jnp.bfloat16)
     out_spec = pl.BlockSpec((step * rows, lanes), lambda i: (i, 0))
-    return pl.pallas_call(
+    return call(
         functools.partial(back_y_kernel, rows),
-        grid=(count // step,),
-        in_specs=[
+        [data, table],
+        [
             pl.BlockSpec((wide, step, part, lanes), lambda i: (0, i, 0, 0)),
             pl.BlockSpec(table.shape, lambda i: (0, 0)),
         ],
+        after,
+        grid=(count // step,),
         out_specs=[out_spec, out_spec],
         out_shape=[shape, shape],
         compiler_params=params(),
         cost_estimate=cost(2 * count * table.size * lanes, 2 * data.size + 4 * count * rows * lanes),
         name="back_y",
-    )(data, table)
+    )
 
 
 def field_kernel(own_ref, recv_ref, table_ref, *out_refs):
@@ -543,7 +580,7 @@
     field_kernel(own_ref, recv_ref, table_ref, out_ref)
 
 
-def field_call(own, recv, table, total, start, rows, so_far):
+def field_call(own, recv, table, total, start, rows, so_far, after=None):
     step = CHANNEL_STEP
     lanes = own.shape[1]
     columns, cells = table.shape
@@ -558,17 +595,19 @@
         in_specs.append(pl.BlockSpec(memory_space=pl.ANY))
         aliases = {3: 0}
         body = field_kernel_into
-    return pl.pallas_call(
+    return call(
         body,
+        [*operands],
+        in_specs,
+        after,
         grid=(count // step,),
-        in_specs=in_specs,
         out_specs=pl.BlockSpec((step * rows, cells), lambda i: (start // step + i, 0)),
         out_shape=jax.ShapeDtypeStruct((total * rows, cells), jnp.bfloat16),
         input_output_aliases=aliases,
         compiler_params=params(),
         cost_estimate=cost(2 * count * rows * columns * cells, 2 * count * rows * (columns + cells)),
         name="field",
-    )(*operands)
+    )
 
 
 def fast_shards(layer_input, output_cotangent, spectral_weight):
@@ -588,39 +627,74 @@
     def flat(field):
         return jnp.transpose(field[0], (0, 2, 1, 3)).reshape(channels * rows, cells)
 
-    def to_modes(field, table, chunks):
-        count = channels // chunks
-        outs = []
-        for start in range(0, channels, count):
-            own, other = plane_call(field, table, start, count, rows)
-            recv = lax.ppermute(other, "narrow", swap)
-            line = line_call(own, recv, forward_y, wide, rows)
-            line = lax.all_to_all(line, "wide", split_axis=0, concat_axis=0, tiled=True)
-            outs.append(spec_call(line, forward_x, local_x))
-        return outs[0] if chunks == 1 else jnp.concatenate(outs, axis=2)
-
-    grad_spec = to_modes(flat(output_cotangent), doubled, GRAD_CHUNKS)
-    input_spec = to_modes(flat(layer_input), plain, INPUT_CHUNKS)
-    kept = grad_spec.shape[0]
+    count = channels // CHUNKS
+    starts = range(0, channels, count)
+    kept = forward_x.shape[0] // 2
     weight = jnp.transpose(spectral_weight[0], (1, 2, 3, 4, 0))
-    dual = dual_call(weight, grad_spec)
+    last = None
+
+    def plane(field, table, start):
+        nonlocal last
+        own, other = plane_call(field, table, start, count, rows, after=last)
+        last = own
+        return own, lax.ppermute(other, "narrow", swap)
+
+    def line(own, recv):
+        nonlocal last
+        last = line_call(own, recv, forward_y, wide, rows, after=last)
+        return lax.all_to_all(last, "wide", split_axis=0, concat_axis=0, tiled=True)
+
+    def spectrum(chunks):
+        nonlocal last
+        last = spec_call(chunks, forward_x, local_x, after=last)
+        return last
+
+    def back_line(start):
+        nonlocal last
+        last = back_x_call(dual, back_x, wide, local_x, pairs, start, count, after=last)
+        return lax.all_to_all(last, "wide", split_axis=0, concat_axis=0, tiled=True)
+
+    def back_plane(block):
+        nonlocal last
+        own, other = back_y_call(block, back_y, rows, after=last)
+        last = own
+        return own, lax.ppermute(other, "narrow", swap)
 
     def both(spec):
         n_rep = lax.axis_size("rep")
         halves = spec.reshape((n_rep, kept // n_rep) + spec.shape[1:])
         return lax.all_to_all(halves, "rep", split_axis=0, concat_axis=0, tiled=True)
 
-    weight_grad = outer_call(both(input_spec), both(grad_spec))
+    grad_field, input_field = flat(output_cotangent), flat(layer_input)
+    half = CHUNKS // 2
+    grad_planes = [plane(grad_field, doubled, start) for start in starts]
+    grad_lines = [line(*both_halves) for both_halves in grad_planes[:-1]]
+    input_planes = [plane(input_field, plain, starts[0])]
+    grad_lines.append(line(*grad_planes[-1]))
+    input_planes += [plane(input_field, plain, start) for start in starts[1:half]]
+    first_spec = spectrum(grad_lines[:half])
+    dual = dual_call(weight, first_spec, 0, None, False, after=last)
+    last = dual
+    input_planes += [plane(input_field, plain, start) for start in starts[half:]]
+    input_lines = [line(*both_halves) for both_halves in input_planes[:half]]
+    second_spec = spectrum(grad_lines[half:])
+    dual = dual_call(weight, second_spec, channels // 2, dual, True, after=last)
+    last = dual
+    both_grad = [both(spec) for spec in (first_spec, second_spec)]
+    blocks = [back_line(start) for start in starts]
+    back_planes = []
+    for at, block in enumerate(blocks):
+        back_planes.append(back_plane(block))
+        if half <= at + half // 2 + 1 and len(input_lines) < CHUNKS:
+            input_lines.append(line(*input_planes[len(input_lines)]))
+    result = None
+    for start, both_halves in zip(starts, back_planes):
+        result = field_call(*both_halves, inverse, channels, start, rows, result, after=last)
+        last = both_halves[0]
+    input_specs = [both(spectrum(input_lines[:half])), both(spectrum(input_lines[half:]))]
+    both_input = jnp.concatenate(input_specs, axis=3)
+    weight_grad = outer_call(both_input, jnp.concatenate(both_grad, axis=3))
     weight_grad = jnp.transpose(weight_grad, (4, 0, 1, 2, 3))
-
-    count = channels // BACK_CHUNKS
-    result = None
-    for start in range(0, channels, count):
-        block = back_x_call(dual, back_x, wide, local_x, pairs, start, count)
-        block = lax.all_to_all(block, "wide", split_axis=0, concat_axis=0, tiled=True)
-        own, other = back_y_call(block, back_y, rows)
-        recv = lax.ppermute(other, "narrow", swap)
-        result = field_call(own, recv, inverse, channels, start, rows, result)
     field = result.reshape(channels, local_y, local_x, cells)
     return (jnp.transpose(field, (0, 2, 1, 3))[None], weight_grad[None])
 

time: 407 us -> 371 us (0.912)
  blocking collectives: 81.6 us -> 8.86 us
  starting transfers between devices: 20.4 us -> 47.4 us
  Pallas kernels: 117 us -> 128 us
  waiting for transfers between devices: 176 us -> 168 us
  local copies, waits for them, and re-layouts: 9.97 us -> 14.3 us
    all_to_all x1 -> x0, blocking collectives: 76.2 us -> none  [to_modes(): line = lax.all_to_all(line, 'wide', split_axis=0, concat_axis=0, tiled=True)]
    all_to_all x2 -> x6, starting transfers between devices: 10.2 us -> 30.8 us  [the longest x4 23.4 us: line(): return lax.all_to_all(last, 'wide', split_axis=0, concat_axis=0, tiled=True)]
    pallas_call x11 -> x21, Pallas kernels: 117 us -> 128 us  [the longest x19 109 us: call(): return pl.pallas_call(without, in_specs=specs, **settings)(*operands, after)]
    ppermute x3 -> x6, waiting for transfers between devices: 124 us -> 115 us  [the longest x4 72 us: plane(): return (own, lax.ppermute(other, 'narrow', swap))]
    unnamed x24 -> x64, local copies, waits for them, and re-layouts: 6.59 us -> 10.7 us
    ppermute x3 -> x6, starting transfers between devices: 5.91 us -> 9.64 us  [the longest x4 7.55 us: plane(): return (own, lax.ppermute(other, 'narrow', swap))]
    all_to_all x1 -> x2, blocking collectives: 5.45 us -> 8.86 us  [both(): lax.all_to_all(halves, 'rep', split_axis=0, concat_axis=0, tiled=True)]
    all_to_all x2 -> x6, waiting for transfers between devices: 51.5 us -> 52.1 us  [the longest x2 34.7 us: back_line(): return lax.all_to_all(last, 'wide', split_axis=0, concat_axis=0, tiled=True)]
  transfers between devices with their start and end apart: 6 -> 14, of which waited for: 3 -> 9; matrix products, arithmetic and copies ran while one was open for 1% -> 1% of each run, Pallas kernels for 12% -> 28%
where the time goes in v2:
time: 371 us; the launch traced here: 369 us
  waiting for transfers between devices  168 us (45%)
  Pallas kernels  128 us (35%)
  starting transfers between devices  47.4 us (13%)
  local copies, waits for them, and re-layouts  14.3 us (4%)
  blocking collectives  8.86 us (2%)
    pallas_call x19, Pallas kernels, call(): return pl.pallas_call(without, in_specs=specs, **settings)(*operands, after)  109 us
    ppermute x4, waiting for transfers between devices, plane(): return (own, lax.ppermute(other, 'narrow', swap))  72 us
    ppermute x2, waiting for transfers between devices, back_plane(): return (own, lax.ppermute(other, 'narrow', swap))  43.1 us
    all_to_all x2, waiting for transfers between devices, back_line(): return lax.all_to_all(last, 'wide', split_axis=0, concat_axis=0, tiled=True)  34.7 us
    all_to_all x4, starting transfers between devices, line(): return lax.all_to_all(last, 'wide', split_axis=0, concat_axis=0, tiled=True)  23.4 us
    pallas_call x2, Pallas kernels, call(): return pl.pallas_call(body, in_specs=in_specs, **settings)(*operands)  19 us
    all_to_all x4, waiting for transfers between devices, line(): return lax.all_to_all(last, 'wide', split_axis=0, concat_axis=0, tiled=True)  17.4 us
    unnamed x64, local copies, waits for them, and re-layouts  10.7 us
  transfers between devices with their start and end apart: 14, of which 9 were waited for; matrix products, arithmetic and copies ran while one was open for 1% of the time, Pallas kernels for 28%

profile of v2, /device:TPU:0, one launch (start us, length us, event | category | flops | bytes accessed | tf_op | source)
XLA Modules:
  0.0 369.1 jit_solution(13734562093735585073)
XLA Ops:
  1.7 6.8 %plane.4 = (bf16[5632,128]{1,0:T(8,128)(2,1)S(1)}, bf16[5632,128]{1,0:T(8,128)(2,1)S(1)}) custom-call(bf16[11264,1024]{1,0:T(8,128)(2,1)} %bitcast.39, bf16[1024,256]{1,0:T(8,128)(2,1)S(1)} %dynamic-slice_bitcast_fusion.4.table_ref.refs_1_), custom_call_target="tpu_custom_call" | custom-call | flops 2952790016 | bytes 14417920 | tf_op jit(solution)/shard_map/plane/pallas_call | solution.py:251
  8.5 3.0 collective-permute-start.1
  11.6 7.1 %plane.5 = (bf16[5632,128]{1,0:T(8,128)(2,1)S(1)}, bf16[5632,128]{1,0:T(8,128)(2,1)S(1)}) custom-call(bf16[11264,1024]{1,0:T(8,128)(2,1)} %bitcast.40, bf16[1024,256]{1,0:T(8,128)(2,1)S(1)} %dynamic-slice_bitcast_fusion.4.table_ref.refs_1_, bf16[5632,128]{1,0:T(8,128)(2,1)S(1)} %get-tuple-element.14.refs_2_.refs_0_), custom_call_target="tpu_custom_call" | custom-call | flops 2952790016 | bytes 14417920 | tf_op jit(solution)/shard_map/plane/pallas_call | solution.py:257
  19.8 23.3 %collective-permute-done.1.refs_1_ = bf16[5632,128]{1,0:T(8,128)(2,1)S(1)} collective-permute-done((bf16[5632,128]{1,0:T(8,128)(2,1)S(1)}, bf16[5632,128]{1,0:T(8,128)(2,1)S(1)}, u32[]{:S(2)}, u32[]{:S(2)}) %collective-permute-start.1) | collective-permute-done | bytes 1441824 | tf_op jit(solution)/shard_map/ppermute | solution.py:640
  43.1 4.6 %line.4.refs_2_ = bf16[8,16,48,128]{3,2,1,0:T(8,128)(2,1)} custom-call(bf16[5632,128]{1,0:T(8,128)(2,1)S(1)} %get-tuple-element.14.refs_2_.refs_0_, bf16[5632,128]{1,0:T(8,128)(2,1)S(1)} %collective-permute-done.1.refs_1_, bf16[768,704]{1,0:T(8,128)(2,1)S(1)} %dynamic-slice_bitcast_fusion.refs_2_, bf16[5632,128]{1,0:T(8,128)(2,1)S(1)} %get-tuple-element.15.refs_3_.refs_0_), custom_call_target="tpu_custom_call" | custom-call | flops 2214592512 | bytes 4456448 | tf_op jit(solution)/shard_map/line/pallas_call | solution.py:257
  48.8 6.2 %all-to-all-start.1 = ((bf16[8,16,48,128]{3,2,1,0:T(8,128)(2,1)}), bf16[8,16,48,128]{3,2,1,0:T(8,128)(2,1)S(1)}, u32[]{:S(2)}, u32[]{:S(2)}) async-start(bf16[8,16,48,128]{3,2,1,0:T(8,128)(2,1)} %line.4.refs_2_), calls=%async_computation.1 | async-start | bytes 3145728 | tf_op jit(solution)/shard_map/all_to_all | solution.py:645
  55.0 1.5 collective-permute-start
  57.6 6.8 %plane.6 = (bf16[5632,128]{1,0:T(8,128)(2,1)S(1)}, bf16[5632,128]{1,0:T(8,128)(2,1)S(1)}) custom-call(bf16[11264,1024]{1,0:T(8,128)(2,1)} %bitcast.41, bf16[1024,256]{1,0:T(8,128)(2,1)S(1)} %dynamic-slice_bitcast_fusion.3.refs_1_, bf16[8,16,48,128]{3,2,1,0:T(8,128)(2,1)S(1)} %copy-done.1), custom_call_target="tpu_custom_call" | custom-call | flops 2952790016 | bytes 14417920 | tf_op jit(solution)/shard_map/plane/pallas_call | solution.py:257
  65.6 21.8 %collective-permute-done.refs_1_ = bf16[5632,128]{1,0:T(8,128)(2,1)S(1)} collective-permute-done((bf16[5632,128]{1,0:T(8,128)(2,1)}, bf16[5632,128]{1,0:T(8,128)(2,1)S(1)}, u32[]{:S(2)}, u32[]{:S(2)}) %collective-permute-start) | collective-permute-done | bytes 1441824 | tf_op jit(solution)/shard_map/ppermute | solution.py:640
  87.4 4.6 %line.5.refs_2_ = bf16[8,16,48,128]{3,2,1,0:T(8,128)(2,1)} custom-call(bf16[5632,128]{1,0:T(8,128)(2,1)S(1)} %copy-done.25, bf16[5632,128]{1,0:T(8,128)(2,1)S(1)} %collective-permute-done.refs_1_, bf16[768,704]{1,0:T(8,128)(2,1)S(1)} %copy-done.10, bf16[5632,128]{1,0:T(8,128)(2,1)S(1)} %get-tuple-element.18.refs_3_.refs_0_), custom_call_target="tpu_custom_call" | custom-call | flops 2214592512 | bytes 4456448 | tf_op jit(solution)/shard_map/line/pallas_call | solution.py:257
  92.0 1.2 copy-done.21
  93.2 5.8 %all-to-all-start = ((bf16[8,16,48,128]{3,2,1,0:T(8,128)(2,1)}), bf16[8,16,48,128]{3,2,1,0:T(8,128)(2,1)}, u32[]{:S(2)}, u32[]{:S(2)}) async-start(bf16[8,16,48,128]{3,2,1,0:T(8,128)(2,1)} %line.5.refs_2_), calls=%async_computation | async-start | bytes 3145728 | tf_op jit(solution)/shard_map/all_to_all | solution.py:645
  99.0 1.5 collective-permute-start.2
  100.5 1.7 spec.4.refs_1_.refs_2_
  102.2 17.5 %dual.2.refs_2_ = f32[24,2,32,192]{3,2,1,0:T(8,128)S(1)} custom-call(bf16[24,2,32,32,192]{4,3,2,1,0:T(8,128)(2,1)} %bitcast.37, bf16[24,2,16,192]{3,2,1,0:T(8,128)(2,1)} %spec.4.refs_1_.refs_2_, bf16[24,2,16,192]{3,2,1,0:T(8,128)(2,1)} %spec.4.refs_1_.refs_2_), custom_call_target="tpu_custom_call" | custom-call | flops 9437184 | bytes 9437184 | tf_op jit(solution)/shard_map/dual/pallas_call | solution.py:257
  119.7 7.7 %plane.7 = (bf16[5632,128]{1,0:T(8,128)(2,1)S(1)}, bf16[5632,128]{1,0:T(8,128)(2,1)}) custom-call(bf16[11264,1024]{1,0:T(8,128)(2,1)} %bitcast.42, bf16[1024,256]{1,0:T(8,128)(2,1)S(1)} %copy-done.3, f32[24,2,32,192]{3,2,1,0:T(8,128)S(1)} %dual.2.refs_2_), custom_call_target="tpu_custom_call" | custom-call | flops 2952790016 | bytes 14417920 | tf_op jit(solution)/shard_map/plane/pallas_call | solution.py:257
  127.4 2.5 collective-permute-done.2.refs_1_
  129.9 4.6 %line.6.refs_2_ = bf16[8,16,48,128]{3,2,1,0:T(8,128)(2,1)} custom-call(bf16[5632,128]{1,0:T(8,128)(2,1)S(1)} %copy-done.22, bf16[5632,128]{1,0:T(8,128)(2,1)S(1)} %collective-permute-done.2.refs_1_, bf16[768,704]{1,0:T(8,128)(2,1)S(1)} %copy-done.11, bf16[5632,128]{1,0:T(8,128)(2,1)S(1)} %get-tuple-element.20.refs_3_.refs_0_), custom_call_target="tpu_custom_call" | custom-call | flops 2214592512 | bytes 4456448 | tf_op jit(solution)/shard_map/line/pallas_call | solution.py:257
  134.5 3.5 all-to-all-start.8
  138.0 2.3 spec.5.refs_1_.refs_3_
  140.4 4.8 %all_to_all.50 = bf16[2,12,2,16,192]{4,3,2,1,0:T(8,128)(2,1)} all-to-all(bf16[2,12,2,16,192]{4,3,2,1,0:T(8,128)(2,1)S(1)} %bitcast.35), channel_id=1, replica_groups=mesh['wide'=8,'narrow'=2,'rep'=2] {'rep'}, dimensions={0} | all-to-all | bytes 589824 | tf_op jit(solution)/shard_map/all_to_all | solution.py:666
  145.2 5.7 %all-to-all-start.4 = ((bf16[8,16,48,128]{3,2,1,0:T(8,128)(2,1)}), bf16[8,16,48,128]{3,2,1,0:T(8,128)(2,1)}, u32[]{:S(2)}, u32[]{:S(2)}) async-start(bf16[8,16,48,128]{3,2,1,0:T(8,128)(2,1)} %line.6.refs_2_), calls=%async_computation.4 | async-start | bytes 3145728 | tf_op jit(solution)/shard_map/all_to_all | solution.py:645
  150.9 17.5 %dual.3.refs_0_.refs_2_ = f32[24,2,32,192]{3,2,1,0:T(8,128)S(1)} custom-call(bf16[24,2,32,32,192]{4,3,2,1,0:T(8,128)(2,1)} %bitcast.38, bf16[24,2,16,192]{3,2,1,0:T(8,128)(2,1)S(1)} %spec.5.refs_1_.refs_3_, f32[24,2,32,192]{3,2,1,0:T(8,128)S(1)} %dual.2.refs_2_, bf16[24,2,16,192]{3,2,1,0:T(8,128)(2,1)S(1)} %spec.5.refs_1_.refs_3_), custom_call_target="tpu_custom_call" | custom-call | flops 9437184 | bytes 9437184 | tf_op jit(solution)/shard_map/dual/pallas_call | solution.py:257
  168.5 2.5 back_x.2.refs_2_
  170.9 17.4 %all-to-all-done.4.refs_0_ = bf16[8,16,48,128]{3,2,1,0:T(8,128)(2,1)} async-done(((bf16[8,16,48,128]{3,2,1,0:T(8,128)(2,1)}), bf16[8,16,48,128]{3,2,1,0:T(8,128)(2,1)}, u32[]{:S(2)}, u32[]{:S(2)}) %all-to-all-start.4) | async-done | bytes 1572896 | tf_op jit(solution)/shard_map/all_to_all | solution.py:645
  188.3 3.6 all-to-all-start.3
  192.0 2.5 back_x.3.refs_2_
  194.4 34.7 %all-to-all-done.3.refs_0_ = bf16[8,16,48,128]{3,2,1,0:T(8,128)(2,1)S(1)} async-done(((bf16[8,16,48,128]{3,2,1,0:T(8,128)(2,1)}), bf16[8,16,48,128]{3,2,1,0:T(8,128)(2,1)S(1)}, u32[]{:S(2)}, u32[]{:S(2)}) %all-to-all-start.3) | async-done | bytes 1572896 | tf_op jit(solution)/shard_map/all_to_all | solution.py:655
  230.3 3.8 %all-to-all-start.2 = ((bf16[8,16,48,128]{3,2,1,0:T(8,128)(2,1)}), bf16[8,16,48,128]{3,2,1,0:T(8,128)(2,1)S(1)}, u32[]{:S(2)}, u32[]{:S(2)}) async-start(bf16[8,16,48,128]{3,2,1,0:T(8,128)(2,1)} %back_x.3.refs_2_), calls=%async_computation.2 | async-start | bytes 3145728 | tf_op jit(solution)/shard_map/all_to_all | solution.py:655
  234.1 1.6 collective-permute-start.3
  235.6 1.3 dynamic-slice_bitcast_fusion.1.refs_1_
  237.0 4.9 %back_y.2 = (bf16[5632,128]{1,0:T(8,128)(2,1)S(1)}, bf16[5632,128]{1,0:T(8,128)(2,1)S(1)}) custom-call(bf16[8,16,48,128]{3,2,1,0:T(8,128)(2,1)S(1)} %copy-done.8, bf16[1408,384]{1,0:T(8,128)(2,1)S(1)} %dynamic-slice_bitcast_fusion.1.refs_1_, bf16[8,16,48,128]{3,2,1,0:T(8,128)(2,1)} %back_x.3.refs_2_), custom_call_target="tpu_custom_call" | custom-call | flops 2214592512 | bytes 4456448 | tf_op jit(solution)/shard_map/back_y/pallas_call | solution.py:257
  243.0 24.4 %collective-permute-done.3.refs_1_ = bf16[5632,128]{1,0:T(8,128)(2,1)S(1)} collective-permute-done((bf16[5632,128]{1,0:T(8,128)(2,1)}, bf16[5632,128]{1,0:T(8,128)(2,1)S(1)}, u32[]{:S(2)}, u32[]{:S(2)}) %collective-permute-start.3) | collective-permute-done | bytes 1441824 | tf_op jit(solution)/shard_map/ppermute | solution.py:640
  267.4 4.6 %line.7.refs_2_ = bf16[8,16,48,128]{3,2,1,0:T(8,128)(2,1)} custom-call(bf16[5632,128]{1,0:T(8,128)(2,1)S(1)} %copy-done.19, bf16[5632,128]{1,0:T(8,128)(2,1)S(1)} %collective-permute-done.3.refs_1_, bf16[768,704]{1,0:T(8,128)(2,1)S(1)} %copy-done.12, bf16[5632,128]{1,0:T(8,128)(2,1)S(1)} %get-tuple-element.22.refs_3_.refs_0_.refs_4_), custom_call_target="tpu_custom_call" | custom-call | flops 2214592512 | bytes 4456448 | tf_op jit(solution)/shard_map/line/pallas_call | solution.py:257
  272.0 1.1 copy-done.5
  273.2 5.6 %all-to-all-start.6 = ((bf16[8,16,48,128]{3,2,1,0:T(8,128)(2,1)}), bf16[8,16,48,128]{3,2,1,0:T(8,128)(2,1)S(1)}, u32[]{:S(2)}, u32[]{:S(2)}) async-start(bf16[8,16,48,128]{3,2,1,0:T(8,128)(2,1)} %line.7.refs_2_), calls=%async_computation.6 | async-start | bytes 3145728 | tf_op jit(solution)/shard_map/all_to_all | solution.py:645
  278.8 1.5 collective-permute-start.5
  280.3 1.4 copy-done.6
  281.7 1.2 copy-done.14
  283.0 4.8 %back_y.3 = (bf16[5632,128]{1,0:T(8,128)(2,1)S(1)}, bf16[5632,128]{1,0:T(8,128)(2,1)S(1)}) custom-call(bf16[8,16,48,128]{3,2,1,0:T(8,128)(2,1)S(1)} %copy-done.6, bf16[1408,384]{1,0:T(8,128)(2,1)S(1)} %copy-done.14, bf16[8,16,48,128]{3,2,1,0:T(8,128)(2,1)} %line.7.refs_2_), custom_call_target="tpu_custom_call" | custom-call | flops 2214592512 | bytes 4456448 | tf_op jit(solution)/shard_map/back_y/pallas_call | solution.py:257
  289.5 3.1 spec.6.refs_2_
  292.6 20.9 %collective-permute-done.5.refs_1_ = bf16[5632,128]{1,0:T(8,128)(2,1)S(1)} collective-permute-done((bf16[5632,128]{1,0:T(8,128)(2,1)}, bf16[5632,128]{1,0:T(8,128)(2,1)S(1)}, u32[]{:S(2)}, u32[]{:S(2)}) %collective-permute-start.5) | collective-permute-done | bytes 1441824 | tf_op jit(solution)/shard_map/ppermute | solution.py:661
  313.5 5.9 %field.2.refs_3_ = bf16[11264,1024]{1,0:T(8,128)(2,1)} custom-call(bf16[5632,128]{1,0:T(8,128)(2,1)S(1)} %get-tuple-element.22.refs_3_.refs_0_.refs_4_, bf16[5632,128]{1,0:T(8,128)(2,1)S(1)} %collective-permute-done.5.refs_1_, bf16[256,1024]{1,0:T(8,128)(2,1)S(1)} %dynamic-slice_bitcast_fusion.2.refs_2_, ...), custom_call_target="tpu_custom_call" | custom-call | flops 2952790016 | bytes 14417920 | tf_op jit(solution)/shard_map/field/pallas_call | solution.py:257
  319.5 22.2 %collective-permute-done.4.refs_1_ = bf16[5632,128]{1,0:T(8,128)(2,1)S(1)} collective-permute-done((bf16[5632,128]{1,0:T(8,128)(2,1)S(1)}, bf16[5632,128]{1,0:T(8,128)(2,1)S(1)}, u32[]{:S(2)}, u32[]{:S(2)}) %collective-permute-start.4) | collective-permute-done | bytes 1441824 | tf_op jit(solution)/shard_map/ppermute | solution.py:661
  341.7 5.9 %field.3 = bf16[11264,1024]{1,0:T(8,128)(2,1)} custom-call(bf16[5632,128]{1,0:T(8,128)(2,1)S(1)} %get-tuple-element.23.refs_3_.refs_0_.refs_2_, bf16[5632,128]{1,0:T(8,128)(2,1)S(1)} %collective-permute-done.4.refs_1_, bf16[256,1024]{1,0:T(8,128)(2,1)S(1)} %dynamic-slice_bitcast_fusion.2.refs_2_, ...), custom_call_target="tpu_custom_call", output_to_operand_aliasing={{}: (3, {})} | custom-call | flops 2952790016 | bytes 14417920 | tf_op jit(solution)/shard_map/field/pallas_call | solution.py:257
  347.6 3.5 all-to-all-start.5
  352.7 4.0 %all_to_all.51 = bf16[2,12,2,16,192]{4,3,2,1,0:T(8,128)(2,1)S(1)} all-to-all(bf16[2,12,2,16,192]{4,3,2,1,0:T(8,128)(2,1)S(1)} %bitcast.36), channel_id=1, replica_groups=mesh['wide'=8,'narrow'=2,'rep'=2] {'rep'}, dimensions={0} | all-to-all | bytes 589824 | tf_op jit(solution)/shard_map/all_to_all | solution.py:666
  356.9 12.2 %outer.1 = f32[12,2,32,32,192]{4,3,2,1,0:T(8,128)} custom-call(bf16[2,12,2,32,192]{4,3,2,1,0:T(8,128)(2,1)S(1)} %pad_maximum_fusion.input_ref, bf16[2,12,2,32,192]{4,3,2,1,0:T(8,128)(2,1)S(1)} %copy-done.4), custom_call_target="tpu_custom_call" | custom-call | flops 37748736 | bytes 28311552 | tf_op jit(solution)/shard_map/outer/pallas_call | solution.py:251
  (74 shorter events, 11.4 us)
Async XLA Ops:
  1.7 9.8 %copy-start.30 = (bf16[2,768,704]{2,1,0:T(8,128)(2,1)S(1)}, bf16[2,768,704]{2,1,0:T(8,128)(2,1)}, u32[]{:S(2)}) copy-start(bf16[2,768,704]{2,1,0:T(8,128)(2,1)} %constant.41.clone) | copy-start | bytes 6488068
  8.5 34.6 %collective-permute-start.1 = (bf16[5632,128]{1,0:T(8,128)(2,1)S(1)}, bf16[5632,128]{1,0:T(8,128)(2,1)S(1)}, u32[]{:S(2)}, u32[]{:S(2)}) collective-permute-start(bf16[5632,128]{1,0:T(8,128)(2,1)S(1)} %get-tuple-element.17), channel_id=1, source_target_pairs={{0,2},{2,0},{1,3},{3,1},{4,6},{6,4},{5,7},{7,5},{8,10},{10,8},{9,1... | collective-permute-start | bytes 4325384 | tf_op jit(solution)/shard_map/ppermute | solution.py:640
  11.6 31.5 %copy-start.9 = (bf16[768,704]{1,0:T(8,128)(2,1)}, bf16[768,704]{1,0:T(8,128)(2,1)S(1)}, u32[]{:S(2)}) copy-start(bf16[768,704]{1,0:T(8,128)(2,1)S(1)} %dynamic-slice_bitcast_fusion.refs_2_) | copy-start | bytes 3244036
  18.7 1.1 copy-start.26
  47.7 1.1 copy-start.24
  48.8 8.8 %copy-start.1 = (bf16[8,16,48,128]{3,2,1,0:T(8,128)(2,1)S(1)}, bf16[8,16,48,128]{3,2,1,0:T(8,128)(2,1)}, u32[]{:S(2)}) copy-start(bf16[8,16,48,128]{3,2,1,0:T(8,128)(2,1)} %line.4.refs_2_) | copy-start | bytes 4718596
  48.8 44.4 %all-to-all-start.1 = ((bf16[8,16,48,128]{3,2,1,0:T(8,128)(2,1)}), bf16[8,16,48,128]{3,2,1,0:T(8,128)(2,1)S(1)}, u32[]{:S(2)}, u32[]{:S(2)}) async-start(bf16[8,16,48,128]{3,2,1,0:T(8,128)(2,1)} %line.4.refs_2_), calls=%async_computation.1 | async-start | bytes 3145728 | tf_op jit(solution)/shard_map/all_to_all | solution.py:645
  55.0 32.4 %collective-permute-start = (bf16[5632,128]{1,0:T(8,128)(2,1)}, bf16[5632,128]{1,0:T(8,128)(2,1)S(1)}, u32[]{:S(2)}, u32[]{:S(2)}) collective-permute-start(bf16[5632,128]{1,0:T(8,128)(2,1)} %copy-done.26), channel_id=1, source_target_pairs={{0,2},{2,0},{1,3},{3,1},{4,6},{6,4},{5,7},{7,5},{8,10},{10,8},{9,1... | collective-permute-start | bytes 4325384 | tf_op jit(solution)/shard_map/ppermute | solution.py:640
  57.6 6.9 %copy-start.2 = (bf16[1024,256]{1,0:T(8,128)(2,1)}, bf16[1024,256]{1,0:T(8,128)(2,1)S(1)}, u32[]{:S(2)}) copy-start(bf16[1024,256]{1,0:T(8,128)(2,1)S(1)} %dynamic-slice_bitcast_fusion.3.refs_1_) | copy-start | bytes 1572868
  57.6 29.8 %copy-start.10 = (bf16[768,704]{1,0:T(8,128)(2,1)S(1)}, bf16[768,704]{1,0:T(8,128)(2,1)}, u32[]{:S(2)}) copy-start(bf16[768,704]{1,0:T(8,128)(2,1)} %copy-done.9) | copy-start | bytes 3244036
  57.6 29.8 %copy-start.25 = (bf16[5632,128]{1,0:T(8,128)(2,1)S(1)}, bf16[5632,128]{1,0:T(8,128)(2,1)}, u32[]{:S(2)}) copy-start(bf16[5632,128]{1,0:T(8,128)(2,1)} %copy-done.24) | copy-start | bytes 4325380
  64.5 1.1 copy-start.23
  92.0 1.2 copy-start.21
  93.2 7.4 %copy-start = (bf16[8,16,48,128]{3,2,1,0:T(8,128)(2,1)S(1)}, bf16[8,16,48,128]{3,2,1,0:T(8,128)(2,1)}, u32[]{:S(2)}) copy-start(bf16[8,16,48,128]{3,2,1,0:T(8,128)(2,1)} %line.5.refs_2_) | copy-start | bytes 4718596
  93.2 7.4 %copy-start.17 = (bf16[48,128]{1,0:T(8,128)(2,1)S(1)}, bf16[48,128]{1,0:T(8,128)(2,1)}, u32[]{:S(2)}) copy-start(bf16[48,128]{1,0:T(8,128)(2,1)} %constant.43.clone.refs_1_) | copy-start | bytes 36868
  93.2 41.3 %all-to-all-start = ((bf16[8,16,48,128]{3,2,1,0:T(8,128)(2,1)}), bf16[8,16,48,128]{3,2,1,0:T(8,128)(2,1)}, u32[]{:S(2)}, u32[]{:S(2)}) async-start(bf16[8,16,48,128]{3,2,1,0:T(8,128)(2,1)} %line.5.refs_2_), calls=%async_computation | async-start | bytes 3145728 | tf_op jit(solution)/shard_map/all_to_all | solution.py:645
  99.0 30.9 %collective-permute-start.2 = (bf16[5632,128]{1,0:T(8,128)(2,1)}, bf16[5632,128]{1,0:T(8,128)(2,1)S(1)}, u32[]{:S(2)}, u32[]{:S(2)}) collective-permute-start(bf16[5632,128]{1,0:T(8,128)(2,1)} %copy-done.23), channel_id=1, source_target_pairs={{0,2},{2,0},{1,3},{3,1},{4,6},{6,4},{5,7},{7,5},{8,10},{10,8},{9,1... | collective-permute-start | bytes 4325384 | tf_op jit(solution)/shard_map/ppermute | solution.py:640
  102.2 17.5 %copy-start.3 = (bf16[1024,256]{1,0:T(8,128)(2,1)S(1)}, bf16[1024,256]{1,0:T(8,128)(2,1)}, u32[]{:S(2)}) copy-start(bf16[1024,256]{1,0:T(8,128)(2,1)} %copy-done.2) | copy-start | bytes 1572868
  119.7 10.2 %copy-start.11 = (bf16[768,704]{1,0:T(8,128)(2,1)S(1)}, bf16[768,704]{1,0:T(8,128)(2,1)}, u32[]{:S(2)}) copy-start(bf16[768,704]{1,0:T(8,128)(2,1)} %copy-done.9) | copy-start | bytes 3244036
  119.7 10.2 %copy-start.22 = (bf16[5632,128]{1,0:T(8,128)(2,1)S(1)}, bf16[5632,128]{1,0:T(8,128)(2,1)}, u32[]{:S(2)}) copy-start(bf16[5632,128]{1,0:T(8,128)(2,1)} %copy-done.21) | copy-start | bytes 4325380
  127.4 7.1 %copy-start.18 = (bf16[5632,128]{1,0:T(8,128)(2,1)}, bf16[5632,128]{1,0:T(8,128)(2,1)S(1)}, u32[]{:S(2)}) copy-start(bf16[5632,128]{1,0:T(8,128)(2,1)S(1)} %get-tuple-element.20.refs_3_.refs_0_) | copy-start | bytes 4325380
  134.5 5.8 %all-to-all-start.8 = ((bf16[2,12,2,16,192]{4,3,2,1,0:T(8,128)(2,1)}), bf16[2,12,2,16,192]{4,3,2,1,0:T(8,128)(2,1)S(1)}, u32[]{:S(2)}, u32[]{:S(2)}) async-start(bf16[2,12,2,16,192]{4,3,2,1,0:T(8,128)(2,1)} %bitcast.23), calls=%async_computation.8 | async-start | bytes 786432 | tf_op jit(solution)/shard_map/all_to_all | solution.py:666
  140.3 4.8 %copy-start.27 = (bf16[2,12,2,16,192]{4,3,2,1,0:T(8,128)(2,1)}, bf16[2,12,2,16,192]{4,3,2,1,0:T(8,128)(2,1)S(1)}, u32[]{:S(2)}) copy-start(bf16[2,12,2,16,192]{4,3,2,1,0:T(8,128)(2,1)S(1)} %all-to-all-done.8) | copy-start | bytes 884740
  145.2 43.1 %all-to-all-start.4 = ((bf16[8,16,48,128]{3,2,1,0:T(8,128)(2,1)}), bf16[8,16,48,128]{3,2,1,0:T(8,128)(2,1)}, u32[]{:S(2)}, u32[]{:S(2)}) async-start(bf16[8,16,48,128]{3,2,1,0:T(8,128)(2,1)} %line.6.refs_2_), calls=%async_computation.4 | async-start | bytes 3145728 | tf_op jit(solution)/shard_map/all_to_all | solution.py:645
  150.9 17.6 %copy-start.15 = (bf16[256,24]{1,0:T(8,128)(2,1)S(1)}, bf16[256,24]{1,0:T(8,128)(2,1)}, u32[]{:S(2)}) copy-start(bf16[256,24]{1,0:T(8,128)(2,1)} %constant.44.clone.refs_1_) | copy-start | bytes 36868
  170.9 21.0 %copy-start.16 = (bf16[256,24]{1,0:T(8,128)(2,1)S(1)}, bf16[256,24]{1,0:T(8,128)(2,1)}, u32[]{:S(2)}) copy-start(bf16[256,24]{1,0:T(8,128)(2,1)} %constant.44.clone.refs_1_) | copy-start | bytes 36868
  188.3 40.8 %all-to-all-start.3 = ((bf16[8,16,48,128]{3,2,1,0:T(8,128)(2,1)}), bf16[8,16,48,128]{3,2,1,0:T(8,128)(2,1)S(1)}, u32[]{:S(2)}, u32[]{:S(2)}) async-start(bf16[8,16,48,128]{3,2,1,0:T(8,128)(2,1)} %back_x.2.refs_2_), calls=%async_computation.3 | async-start | bytes 3145728 | tf_op jit(solution)/shard_map/all_to_all | solution.py:655
  229.1 1.1 copy-start.7
  230.3 41.7 %all-to-all-start.2 = ((bf16[8,16,48,128]{3,2,1,0:T(8,128)(2,1)}), bf16[8,16,48,128]{3,2,1,0:T(8,128)(2,1)S(1)}, u32[]{:S(2)}, u32[]{:S(2)}) async-start(bf16[8,16,48,128]{3,2,1,0:T(8,128)(2,1)} %back_x.3.refs_2_), calls=%async_computation.2 | async-start | bytes 3145728 | tf_op jit(solution)/shard_map/all_to_all | solution.py:655
  234.1 2.9 copy-start.8
  234.1 33.4 %collective-permute-start.3 = (bf16[5632,128]{1,0:T(8,128)(2,1)}, bf16[5632,128]{1,0:T(8,128)(2,1)S(1)}, u32[]{:S(2)}, u32[]{:S(2)}) collective-permute-start(bf16[5632,128]{1,0:T(8,128)(2,1)} %get-tuple-element.21), channel_id=1, source_target_pairs={{0,2},{2,0},{1,3},{3,1},{4,6},{6,4},{5,7},{7,5},{8,10},{10,8},{9,1... | collective-permute-start | bytes 4325384 | tf_op jit(solution)/shard_map/ppermute | solution.py:640
  237.0 4.9 %copy-start.13 = (bf16[1408,384]{1,0:T(8,128)(2,1)}, bf16[1408,384]{1,0:T(8,128)(2,1)S(1)}, u32[]{:S(2)}) copy-start(bf16[1408,384]{1,0:T(8,128)(2,1)S(1)} %dynamic-slice_bitcast_fusion.1.refs_1_) | copy-start | bytes 3244036
  237.0 30.4 %copy-start.12 = (bf16[768,704]{1,0:T(8,128)(2,1)S(1)}, bf16[768,704]{1,0:T(8,128)(2,1)}, u32[]{:S(2)}) copy-start(bf16[768,704]{1,0:T(8,128)(2,1)} %copy-done.9) | copy-start | bytes 3244036
  237.0 30.4 %copy-start.19 = (bf16[5632,128]{1,0:T(8,128)(2,1)S(1)}, bf16[5632,128]{1,0:T(8,128)(2,1)}, u32[]{:S(2)}) copy-start(bf16[5632,128]{1,0:T(8,128)(2,1)} %copy-done.18) | copy-start | bytes 4325380
  241.9 1.1 copy-start.20
  272.0 1.1 copy-start.5
  273.2 74.4 %all-to-all-start.6 = ((bf16[8,16,48,128]{3,2,1,0:T(8,128)(2,1)}), bf16[8,16,48,128]{3,2,1,0:T(8,128)(2,1)S(1)}, u32[]{:S(2)}, u32[]{:S(2)}) async-start(bf16[8,16,48,128]{3,2,1,0:T(8,128)(2,1)} %line.7.refs_2_), calls=%async_computation.6 | async-start | bytes 3145728 | tf_op jit(solution)/shard_map/all_to_all | solution.py:645
  278.8 34.7 %collective-permute-start.5 = (bf16[5632,128]{1,0:T(8,128)(2,1)}, bf16[5632,128]{1,0:T(8,128)(2,1)S(1)}, u32[]{:S(2)}, u32[]{:S(2)}) collective-permute-start(bf16[5632,128]{1,0:T(8,128)(2,1)} %copy-done.20), channel_id=1, source_target_pairs={{0,2},{2,0},{1,3},{3,1},{4,6},{6,4},{5,7},{7,5},{8,10},{10,8},{9,1... | collective-permute-start | bytes 4325384 | tf_op jit(solution)/shard_map/ppermute | solution.py:661
  280.3 1.4 copy-start.6
  281.7 1.2 copy-start.14
  283.0 5.4 %copy-start.31 = (bf16[2,256,1024]{2,1,0:T(8,128)(2,1)S(1)}, bf16[2,256,1024]{2,1,0:T(8,128)(2,1)}, u32[]{:S(2)}) copy-start(bf16[2,256,1024]{2,1,0:T(8,128)(2,1)} %constant.40.clone) | copy-start | bytes 3145732
  283.0 5.5 %copy-start.28 = (bf16[2,12,2,16,192]{4,3,2,1,0:T(8,128)(2,1)S(1)}, bf16[2,12,2,16,192]{4,3,2,1,0:T(8,128)(2,1)}, u32[]{:S(2)}) copy-start(bf16[2,12,2,16,192]{4,3,2,1,0:T(8,128)(2,1)} %copy-done.27) | copy-start | bytes 884740
  283.0 5.5 %copy-start.29 = (bf16[2,12,2,16,192]{4,3,2,1,0:T(8,128)(2,1)S(1)}, bf16[2,12,2,16,192]{4,3,2,1,0:T(8,128)(2,1)}, u32[]{:S(2)}) copy-start(bf16[2,12,2,16,192]{4,3,2,1,0:T(8,128)(2,1)} %all_to_all.50) | copy-start | bytes 884740
  287.8 53.8 %collective-permute-start.4 = (bf16[5632,128]{1,0:T(8,128)(2,1)S(1)}, bf16[5632,128]{1,0:T(8,128)(2,1)S(1)}, u32[]{:S(2)}, u32[]{:S(2)}) collective-permute-start(bf16[5632,128]{1,0:T(8,128)(2,1)S(1)} %get-tuple-element.24), channel_id=1, source_target_pairs={{0,2},{2,0},{1,3},{3,1},{4,6},{6,4},{5,7},{7,5},{8,10},{10,8},{9,1... | collective-permute-start | bytes 4325384 | tf_op jit(solution)/shard_map/ppermute | solution.py:661
  347.6 5.1 %all-to-all-start.5 = ((bf16[2,12,2,16,192]{4,3,2,1,0:T(8,128)(2,1)}), bf16[2,12,2,16,192]{4,3,2,1,0:T(8,128)(2,1)S(1)}, u32[]{:S(2)}, u32[]{:S(2)}) async-start(bf16[2,12,2,16,192]{4,3,2,1,0:T(8,128)(2,1)} %bitcast.21), calls=%async_computation.5 | async-start | bytes 786432 | tf_op jit(solution)/shard_map/all_to_all | solution.py:666
  352.0 4.9 %copy-start.4 = (bf16[2,12,2,32,192]{4,3,2,1,0:T(8,128)(2,1)S(1)}, bf16[2,12,2,32,192]{4,3,2,1,0:T(8,128)(2,1)}, u32[]{:S(2)}) copy-start(bf16[2,12,2,32,192]{4,3,2,1,0:T(8,128)(2,1)} %pad_maximum_fusion.1.grad_ref) | copy-start | bytes 1769476
